TPU v7x, 128 devices: a whole 4x4x4 slice. The times are simulated.
128 devices in a mesh: cell: 8 (over z, core), tile: 16 (over x, y).
Axes of the slice: x: 4, y: 4, z: 4, core: 2. Of those that a mesh axis runs over, the one named last changes fastest.
Arguments:
- gaussians: float32 [59, 1048576], P(None, ('cell', 'tile'))
- send_index: int32 [128, 128, 128], P(('cell', 'tile')), may hold values from 0 to 8191, as said below
- tile_slots: int32 [4096, 4, 256], P(('cell', 'tile')), may hold values from 0 to 16383, as said below
- block_count: int32 [4096], P(('cell', 'tile')), may hold values from 1 to 4, as said below
- cotangent: float32 [3, 4096, 256], P(None, ('cell', 'tile')), may hold values from -6 to 6
Outputs:
- image: float32 [3, 4096, 256], P(None, ('cell', 'tile'))
- sh_grad: float32 [48, 1048576], P(None, ('cell', 'tile'))
Inputs may be any that keep to these rules, and one draw needn't show every extreme that they name: `block_count`: every tile has 1 to 4 live blocks, and some tile has exactly 4. `send_index`: a local Gaussian index of the owner. `tile_slots`: a slot of the tile's renderer.
All inputs are finite; a program needn't handle non-finite values.
Results may differ from a plain program's by a relative error of at most 0.0003.
Values sent between devices are 32-bit elements; how exact they have to be, the bound alone decides.
No kernel may reach another device: no remote copies, remote signals or barrier semaphores. Data moves between devices by JAX's collectives and lax.ppermute only.
A program may use at most 128 MiB of HBM per device.

v0:
```python
import jax
import jax.numpy as jnp
from jax import lax
from jax.sharding import PartitionSpec as P

TILE_PIX = 256
BLOCKS = 4


FOCAL_LENGTH = 256.0
CENTRE_SHIFT = 128.0
BLUR_TERM = 0.3
HARM_ZERO = 0.28209479177387814
HARM_ONE = 0.4886025119029199
HARM_TWO = (
    1.0925484305920792,
    -1.0925484305920792,
    0.31539156525252005,
    -1.0925484305920792,
    0.5462742152960396,
)
HARM_THREE = (
    -0.5900435899266435,
    2.890611442640554,
    -0.4570457994644658,
    0.3731763325901154,
    -0.4570457994644658,
    1.445305721320277,
    -0.5900435899266435,
)


def sh_basis(mean_x, mean_y, mean_z):
    inverse_norm = 1.0 / jnp.sqrt(mean_x * mean_x + mean_y * mean_y + mean_z * mean_z)
    unit_x = mean_x * inverse_norm
    unit_y = mean_y * inverse_norm
    unit_z = mean_z * inverse_norm
    square_x = unit_x * unit_x
    square_y = unit_y * unit_y
    square_z = unit_z * unit_z
    return jnp.stack(
        [
            HARM_ZERO * jnp.ones_like(unit_x),
            -HARM_ONE * unit_y,
            HARM_ONE * unit_z,
            -HARM_ONE * unit_x,
            HARM_TWO[0] * unit_x * unit_y,
            HARM_TWO[1] * unit_y * unit_z,
            HARM_TWO[2] * (2.0 * square_z - square_x - square_y),
            HARM_TWO[3] * unit_x * unit_z,
            HARM_TWO[4] * (square_x - square_y),
            HARM_THREE[0] * unit_y * (3.0 * square_x - square_y),
            HARM_THREE[1] * unit_x * unit_y * unit_z,
            HARM_THREE[2] * unit_y * (4.0 * square_z - square_x - square_y),
            HARM_THREE[3] * unit_z * (2.0 * square_z - 3.0 * square_x - 3.0 * square_y),
            HARM_THREE[4] * unit_x * (4.0 * square_z - square_x - square_y),
            HARM_THREE[5] * unit_z * (square_x - square_y),
            HARM_THREE[6] * unit_x * (square_x - 3.0 * square_y),
        ]
    )


def project(params):
    mean_x, mean_y, mean_z = (params[0], params[1], params[2])
    scales = jnp.exp(params[3:6])
    quat_norm = jnp.sqrt(jnp.sum(params[6:10] * params[6:10], axis=0))
    quat_w = params[6] / quat_norm
    quat_x = params[7] / quat_norm
    quat_y = params[8] / quat_norm
    quat_z = params[9] / quat_norm
    rotation = [
        [
            1.0 - 2.0 * (quat_y * quat_y + quat_z * quat_z),
            2.0 * (quat_x * quat_y - quat_w * quat_z),
            2.0 * (quat_x * quat_z + quat_w * quat_y),
        ],
        [
            2.0 * (quat_x * quat_y + quat_w * quat_z),
            1.0 - 2.0 * (quat_x * quat_x + quat_z * quat_z),
            2.0 * (quat_y * quat_z - quat_w * quat_x),
        ],
        [
            2.0 * (quat_x * quat_z - quat_w * quat_y),
            2.0 * (quat_y * quat_z + quat_w * quat_x),
            1.0 - 2.0 * (quat_x * quat_x + quat_y * quat_y),
        ],
    ]
    scaled = [[rotation[row][col] * scales[col] for col in range(3)] for row in range(3)]
    sigma = [
        [sum((scaled[row][inner] * scaled[col][inner] for inner in range(3))) for col in range(3)]
        for row in range(3)
    ]
    inverse_depth = 1.0 / mean_z
    jac_diag = FOCAL_LENGTH * inverse_depth
    jac_first = -FOCAL_LENGTH * mean_x * inverse_depth * inverse_depth
    jac_second = -FOCAL_LENGTH * mean_y * inverse_depth * inverse_depth
    upper_row = [jac_diag * sigma[0][col] + jac_first * sigma[2][col] for col in range(3)]
    lower_row = [jac_diag * sigma[1][col] + jac_second * sigma[2][col] for col in range(3)]
    entry_a = upper_row[0] * jac_diag + upper_row[2] * jac_first + BLUR_TERM
    entry_b = upper_row[1] * jac_diag + upper_row[2] * jac_second
    entry_c = lower_row[1] * jac_diag + lower_row[2] * jac_second + BLUR_TERM
    determinant = entry_a * entry_c - entry_b * entry_b
    centre_u = FOCAL_LENGTH * mean_x * inverse_depth + CENTRE_SHIFT
    centre_v = FOCAL_LENGTH * mean_y * inverse_depth + CENTRE_SHIFT
    opacity = 1.0 / (1.0 + jnp.exp(-params[10]))
    basis = sh_basis(mean_x, mean_y, mean_z)
    coefs = params[11:59].reshape(3, 16, -1)
    colour = 0.5 + jnp.sum(coefs * basis[None], axis=1)
    attributes = jnp.stack(
        [
            centre_u,
            centre_v,
            entry_c / determinant,
            -entry_b / determinant,
            entry_a / determinant,
            opacity,
            colour[0],
            colour[1],
            colour[2],
        ]
    )
    return (attributes, basis)


def render_block(attr_rows, slot_ids, tile_ids, live, cot_part, log_trans):
    picked = jnp.moveaxis(attr_rows[slot_ids], 2, 0)
    local_tile = tile_ids % 256
    pixel = jnp.arange(256, dtype=jnp.int32)
    pos_x = (
        (16 * (local_tile % 16))[:, None].astype(jnp.float32)
        + (pixel % 16).astype(jnp.float32)[None, :]
        + 0.5
    )
    pos_y = (
        (16 * (local_tile // 16))[:, None].astype(jnp.float32)
        + (pixel // 16).astype(jnp.float32)[None, :]
        + 0.5
    )
    delta_x = pos_x[:, :, None] - picked[0][:, None, :]
    delta_y = pos_y[:, :, None] - picked[1][:, None, :]
    power = -0.5 * (
        picked[2][:, None, :] * delta_x * delta_x
        + 2.0 * picked[3][:, None, :] * delta_x * delta_y
        + picked[4][:, None, :] * delta_y * delta_y
    )
    alpha = picked[5][:, None, :] * jnp.exp(power) * live[:, None, None]
    log_keep = jnp.log1p(-alpha)
    order_index = jnp.arange(slot_ids.shape[1], dtype=jnp.int32)
    strictly_before = (order_index[:, None] < order_index[None, :]).astype(jnp.float32)
    earlier = jnp.einsum("npg,gh->nph", log_keep, strictly_before, precision=lax.Precision.HIGHEST)
    weight = alpha * jnp.exp(log_trans[:, :, None] + earlier)
    colour_part = jnp.einsum("npg,cng->cnp", weight, picked[6:9], precision=lax.Precision.HIGHEST)
    colour_grad = jnp.einsum("npg,cnp->cng", weight, cot_part, precision=lax.Precision.HIGHEST)
    return (log_trans + jnp.sum(log_keep, axis=2), colour_part, colour_grad)


def send_ahead(buffer):
    rows = buffer.shape[0]
    arrived = lax.all_to_all(buffer, ("cell", "tile"), split_axis=1, concat_axis=1, tiled=True)
    return arrived.reshape(rows, -1)


def send_back(buffer):
    rows = buffer.shape[0]
    arrived = lax.all_to_all(buffer, ("cell", "tile"), split_axis=1, concat_axis=1, tiled=True)
    return arrived.reshape(rows, -1)


def per_device(gaussians, send_index, tile_slots, block_count, cotangent):
    peers = lax.axis_size(("cell", "tile"))
    rank = lax.axis_index(("cell", "tile"))
    owned = gaussians.shape[1]
    width = send_index.shape[2]
    tile_count = tile_slots.shape[0]
    flat_ids = send_index.reshape(-1)
    chosen_rows = jnp.transpose(jnp.transpose(gaussians)[flat_ids])
    received = send_ahead(chosen_rows.reshape(gaussians.shape[0], peers, width))
    attributes, unused_basis = project(received)
    basis = sh_basis(gaussians[0], gaussians[1], gaussians[2])
    slot_total = attributes.shape[1]
    attr_rows = jnp.transpose(attributes)
    tile_ids = rank * tile_count + jnp.arange(tile_count, dtype=jnp.int32)
    log_trans = jnp.zeros((tile_count, TILE_PIX), jnp.float32)
    picture = jnp.zeros((3, tile_count, TILE_PIX), jnp.float32)
    block_grads = []
    for block in range(BLOCKS):
        alive = (block_count > block).astype(jnp.float32)
        log_trans, colour_part, colour_grad = render_block(
            attr_rows, tile_slots[:, block], tile_ids, alive, cotangent, log_trans
        )
        picture = picture + colour_part
        block_grads.append(colour_grad)
    entry_grad = jnp.stack(block_grads, axis=2)
    entry_rows = jnp.transpose(entry_grad.reshape(3, -1))
    slot_rows = jnp.zeros((slot_total, 3), jnp.float32).at[tile_slots.reshape(-1)].add(entry_rows)
    slot_grad = jnp.transpose(slot_rows)
    returned = send_back(slot_grad.reshape(3, peers, width))
    owned_rows = jnp.zeros((owned, 3), jnp.float32).at[flat_ids].add(jnp.transpose(returned))
    color_grad = jnp.transpose(owned_rows)
    sh_grad = (basis[None] * color_grad[:, None]).reshape(48, owned)
    return (picture, sh_grad)


def solution(mesh):
    placed = (
        P(None, ("cell", "tile")),
        P(("cell", "tile"), None, None),
        P(("cell", "tile"), None, None),
        P(("cell", "tile")),
        P(None, ("cell", "tile"), None),
    )
    return jax.shard_map(
        per_device,
        mesh=mesh,
        in_specs=placed,
        out_specs=(P(None, ("cell", "tile"), None), P(None, ("cell", "tile"))),
        check_vma=False,
    )
```

profile of v0, /device:TPU:1, one launch (start us, length us, event | category | flops | bytes accessed | tf_op | source)
XLA Modules:
  0.0 755.1 jit_solution(10860263204392475081)
XLA Ops:
  2.2 3.9 copy.118
  6.1 56.9 %gather_fusion = f32[16384,59]{1,0:T(8,128)} fusion(f32[8192,59]{1,0:T(8,128)} %bitcast.230, s32[16384]{0:T(1024)S(1)} %broadcast_clamp_fusion), kind=kCustom, calls=%fused_computation | custom fusion | bytes 7798784 | tf_op jit(solution)/shard_map/gather | solution.py:176
  63.0 7.0 copy.119
  70.0 12.0 %all-to-all-start = ((f32[59,128,128]{2,0,1:T(8,128)}), f32[59,128,128]{2,0,1:T(8,128)}, u32[]{:S(2)}, u32[]{:S(2)}) async-start(f32[59,128,128]{2,0,1:T(8,128)} %copy.119), calls=%async_computation | async-start | bytes 8388608 | tf_op jit(solution)/shard_map/all_to_all | solution.py:159
  82.3 1.5 subtract_multiply_fusion.31
  88.6 2.1 stack.25
  91.6 42.7 %all-to-all-done = f32[59,128,128]{2,0,1:T(8,128)} async-done(((f32[59,128,128]{2,0,1:T(8,128)}), f32[59,128,128]{2,0,1:T(8,128)}, u32[]{:S(2)}, u32[]{:S(2)}) %all-to-all-start) | async-done | bytes 3866656 | tf_op jit(solution)/shard_map/all_to_all | solution.py:159
  134.3 1.4 fusion.54
  138.7 2.4 subtract_multiply_fusion.24
  141.1 2.9 multiply_multiply_fusion.2
  144.1 2.9 multiply_multiply_fusion.3
  147.6 2.4 slice.253
  150.0 2.7 copy.129
  152.7 2.9 reshape.1258
  156.2 4.6 stack.22
  160.8 1.9 multiply_reduce_fusion
  162.8 3.0 fusion.86
  167.4 2.1 stack.23
  169.5 4.7 copy.130
  174.1 31.2 %gather_fusion.1 = f32[8192,9]{1,0:T(8,128)} fusion(f32[16384,9]{1,0:T(8,128)} %bitcast.226, s32[8192]{0:T(1024)S(1)} %copy-done.8), kind=kCustom, calls=%fused_computation.1 | custom fusion | bytes 622592 | tf_op jit(solution)/shard_map/gather | solution.py:126
  205.4 3.2 copy.132
  208.8 8.6 %fusion.27 = f32[32,256]{1,0:T(8,128)S(1)} fusion(f32[32]{0:T(128)S(1)} %get-tuple-element.113, f32[32,256]{1,0:T(8,128)S(1)} %bitcast.298, f32[32,256]{1,0:T(8,128)S(1)} %bitcast.300, f32[32,256]{1,0:T(8,128)S(1)} %copy-done.9, f32[32,256]{1,0:T(8,128)S(1)} %bitcast.302, f32[32,256]{1,0:T(8,128)S(1)} %bitcast.304, f32[32,256]{1,0:T(8,128)S(1)} %copy-done.10, ...), kind=kLoop, calls=%fused_computation.65 | loop fusion | flops 31449088 | bytes 295040 | tf_op jit(solution)/shard_map/reduce_sum | solution.py:154
  217.4 16.9 %exponential_multiply_fusion.3 = f32[32,256,256]{2,1,0:T(8,128)} fusion(f32[32]{0:T(128)S(1)} %get-tuple-element.113, f32[32,256]{1,0:T(8,128)S(1)} %bitcast.299, f32[32,256]{1,0:T(8,128)S(1)} %bitcast.301, f32[32,256]{1,0:T(8,128)S(1)} %copy-done.9, f32[32,256]{1,0:T(8,128)S(1)} %bitcast.303, f32[32,256]{1,0:T(8,128)S(1)} %bitcast.305, ...), kind=kOutput, calls=%fused_computation.63 | convolution fusion | flops 6501236736 | bytes 8650880 | tf_op jit(solution)/shard_map/npg,gh->nph/dot_general | solution.py:150
  234.4 31.3 %gather_fusion.4 = f32[8192,9]{1,0:T(8,128)} fusion(f32[16384,9]{1,0:T(8,128)} %bitcast.227, s32[8192]{0:T(1024)S(1)} %copy-done.7), kind=kCustom, calls=%fused_computation.4 | custom fusion | bytes 622592 | tf_op jit(solution)/shard_map/gather | solution.py:126
  265.7 2.8 copy.138
  268.7 31.3 %gather_fusion.3 = f32[8192,9]{1,0:T(8,128)} fusion(f32[16384,9]{1,0:T(8,128)} %bitcast.228, s32[8192]{0:T(1024)S(1)} %copy-done.6), kind=kCustom, calls=%fused_computation.3 | custom fusion | bytes 622592 | tf_op jit(solution)/shard_map/gather | solution.py:126
  300.0 2.8 copy.136
  303.1 31.3 %gather_fusion.2 = f32[8192,9]{1,0:T(8,128)} fusion(f32[16384,9]{1,0:T(8,128)} %bitcast.229, s32[8192]{0:T(1024)S(1)} %broadcast_clamp_fusion.3), kind=kCustom, calls=%fused_computation.2 | custom fusion | bytes 622592 | tf_op jit(solution)/shard_map/gather | solution.py:126
  334.4 2.8 copy.134
  337.4 10.2 %fusion.67 = f32[32,3,256]{2,1,0:T(4,128)S(1)} fusion(f32[32,256,256]{2,1,0:T(8,128)} %exponential_multiply_fusion.3, f32[9,32,256]{2,0,1:T(8,128)S(1)} %bitcast.242), kind=kOutput, calls=%fused_computation.114 | convolution fusion | flops 75497472 | bytes 8617984 | tf_op jit(solution)/shard_map/npg,cng->cnp/dot_general | solution.py:152
  347.6 7.8 %convolution_bitcast_fusion.3 = f32[3,32,1,256]{3,0,1,2:T(4,128)S(1)} fusion(f32[32,256,256]{2,1,0:T(8,128)} %exponential_multiply_fusion.3, f32[3,32,256]{2,1,0:T(8,128)S(1)} %copy-done), kind=kOutput, calls=%fused_computation.89 | convolution fusion | flops 75497472 | bytes 8585216 | tf_op jit(solution)/shard_map/npg,cnp->cng/dot_general | solution.py:153
  355.5 15.5 %exponential_multiply_fusion.2 = f32[32,256,256]{2,1,0:T(8,128)S(1)} fusion(f32[32,256]{1,0:T(8,128)S(1)} %fusion.27, f32[32]{0:T(128)S(1)} %get-tuple-element.112, f32[32,256]{1,0:T(8,128)S(1)} %bitcast.286, f32[32,256]{1,0:T(8,128)S(1)} %bitcast.288, f32[32,256]{1,0:T(8,128)S(1)} %copy-done.9, f32[32,256]{1,0:T(8,128)S(1)} %bitcast.290, ...), kind=kOutput, calls=%fused_computation.61 | convolution fusion | flops 6503333888 | bytes 8683648 | tf_op jit(solution)/shard_map/npg,gh->nph/dot_general | solution.py:150
  371.0 16.4 %fusion.31 = (f32[32,256]{1,0:T(8,128)S(1)}, f32[32,256]{1,0:T(8,128)S(1)}) fusion(f32[32]{0:T(128)S(1)} %get-tuple-element.114, f32[32,256]{1,0:T(8,128)S(1)} %bitcast.274, f32[32,256]{1,0:T(8,128)S(1)} %bitcast.276, f32[32,256]{1,0:T(8,128)S(1)} %copy-done.9, f32[32,256]{1,0:T(8,128)S(1)} %bitcast.278, f32[32,256]{1,0:T(8,128)S(1)} %bitcast.280, ...), kind=kLoop, calls=%fused_computation.69 | loop fusion | flops 62898176 | bytes 524544 | tf_op jit(solution)/shard_map/reduce_sum | solution.py:154
  387.4 15.8 %exponential_multiply_fusion = f32[32,256,256]{2,1,0:T(8,128)S(1)} fusion(f32[32,256]{1,0:T(8,128)S(1)} %get-tuple-element.22, f32[32]{0:T(128)S(1)} %get-tuple-element.111, f32[32,256]{1,0:T(8,128)S(1)} %bitcast.267, f32[32,256]{1,0:T(8,128)S(1)} %bitcast.268, f32[32,256]{1,0:T(8,128)S(1)} %bitcast.269, f32[32,256]{1,0:T(8,128)S(1)} %bitcast.270, ...), kind=kOutput, calls=%fused_computation.55 | convolution fusion | flops 6503333888 | bytes 8683648 | tf_op jit(solution)/shard_map/npg,gh->nph/dot_general | solution.py:150
  403.2 4.5 convolution_bitcast_fusion
  407.7 4.5 convolution_bitcast_fusion.2
  412.2 15.9 %exponential_multiply_fusion.1 = f32[32,256,256]{2,1,0:T(8,128)S(1)} fusion(f32[32,256]{1,0:T(8,128)S(1)} %get-tuple-element.23, f32[32]{0:T(128)S(1)} %get-tuple-element.114, f32[32,256]{1,0:T(8,128)S(1)} %bitcast.275, f32[32,256]{1,0:T(8,128)S(1)} %bitcast.277, f32[32,256]{1,0:T(8,128)S(1)} %copy-done.9, f32[32,256]{1,0:T(8,128)S(1)} %bitcast.279, ...), kind=kOutput, calls=%fused_computation.59 | convolution fusion | flops 6503333888 | bytes 8683648 | tf_op jit(solution)/shard_map/npg,gh->nph/dot_general | solution.py:150
  428.1 4.5 convolution_bitcast_fusion.1
  432.7 7.1 convolution_add_fusion.2
  439.7 7.3 convolution_add_fusion.1
  447.7 8.6 %copy.144 = f32[32768,3]{1,0:T(8,128)} copy(f32[32768,3]{0,1:T(4,128)S(1)} %bitcast.238) | data formatting | bytes 786432 | tf_op jit(solution)/shard_map/transpose | solution.py:194
  456.3 177.9 %scatter_custom_fusion = f32[16384,3]{1,0:T(8,128)} fusion(s32[32768]{0:T(1024)} %bitcast.260, f32[32768,3]{1,0:T(8,128)} %copy.144, f32[]{:T(128)} %constant.156.clone.1), kind=kCustom, calls=%fused_computation.71 | custom fusion | flops 98304 | bytes 197120 | tf_op jit(solution)/shard_map/scatter-add | solution.py:195
  634.2 5.9 copy.145
  640.1 4.6 all-to-all-start.1
  644.7 10.2 %fusion.53 = f32[3,32,256]{2,0,1:T(4,128)S(1)} fusion(f32[32,3,256]{2,1,0:T(4,128)S(1)} %convolution_add_fusion.1, f32[32,256,256]{2,1,0:T(8,128)} %copy-done.1, f32[9,32,256]{2,0,1:T(8,128)S(1)} %bitcast.240), kind=kOutput, calls=%fused_computation.91 | convolution fusion | flops 75522048 | bytes 8749056 | tf_op jit(solution)/shard_map/npg,cng->cnp/dot_general | solution.py:152
  655.7 5.0 copy.146
  660.7 89.8 %scatter_custom_fusion.1 = f32[8192,3]{1,0:T(8,128)} fusion(s32[16384]{0:T(1024)} %bitcast.256, f32[16384,3]{1,0:T(8,128)} %copy.146, f32[]{:T(128)} %constant.156.clone.1), kind=kCustom, calls=%fused_computation.84 | custom fusion | flops 49152 | bytes 98816 | tf_op jit(solution)/shard_map/scatter-add | solution.py:198
  750.5 2.8 copy.147
  (89 shorter events, 16.9 us)
Async XLA Ops:
  0.6 347.0 %copy-start = (f32[3,32,256]{2,1,0:T(8,128)S(1)}, f32[3,32,256]{2,1,0:T(8,128)}, u32[]{:S(2)}) copy-start(f32[3,32,256]{2,1,0:T(8,128)} %param.9) | copy-start | bytes 294916
  1.6 0.6 copy-start.5
  63.0 18.9 %copy-start.4 = (s32[32,4,256]{2,1,0:T(4,128)S(1)}, s32[32,4,256]{2,1,0:T(4,128)}, u32[]{:S(2)}) copy-start(s32[32,4,256]{2,1,0:T(4,128)} %param.7) | copy-start | bytes 393220
  63.0 20.8 %copy-start.11 = (s32[32]{0:T(128)S(1)}, s32[32]{0:T(128)}, u32[]{:S(2)}) copy-start(s32[32]{0:T(128)} %param.8) | copy-start | bytes 388
  70.0 64.3 %all-to-all-start = ((f32[59,128,128]{2,0,1:T(8,128)}), f32[59,128,128]{2,0,1:T(8,128)}, u32[]{:S(2)}, u32[]{:S(2)}) async-start(f32[59,128,128]{2,0,1:T(8,128)} %copy.119), calls=%async_computation | async-start | bytes 8388608 | tf_op jit(solution)/shard_map/all_to_all | solution.py:159
  138.7 8.2 %copy-start.3 = (f32[1,128,128]{2,1,0:T(8,128)}, f32[1,128,128]{2,1,0:T(8,128)S(1)}, u32[]{:S(2)}) copy-start(f32[1,128,128]{2,1,0:T(8,128)S(1)} %get-tuple-element.87) | copy-start | bytes 196612
  162.8 11.4 %copy-start.8 = (s32[8192]{0:T(1024)S(1)}, s32[8192]{0:T(1024)}, u32[]{:S(2)}) copy-start(s32[8192]{0:T(1024)} %broadcast_clamp_fusion.4) | copy-start | bytes 98308
  174.1 34.6 %copy-start.9 = (f32[32,256]{1,0:T(8,128)S(1)}, f32[32,256]{1,0:T(8,128)}, u32[]{:S(2)}) copy-start(f32[32,256]{1,0:T(8,128)} %add_add_fusion.2) | copy-start | bytes 98308
  174.1 34.7 %copy-start.10 = (f32[32,256]{1,0:T(8,128)S(1)}, f32[32,256]{1,0:T(8,128)}, u32[]{:S(2)}) copy-start(f32[32,256]{1,0:T(8,128)} %add_add_fusion.3) | copy-start | bytes 98308
  217.4 17.0 %copy-start.7 = (s32[8192]{0:T(1024)S(1)}, s32[8192]{0:T(1024)}, u32[]{:S(2)}) copy-start(s32[8192]{0:T(1024)} %broadcast_clamp_fusion.1) | copy-start | bytes 98308
  234.4 34.4 %copy-start.6 = (s32[8192]{0:T(1024)S(1)}, s32[8192]{0:T(1024)}, u32[]{:S(2)}) copy-start(s32[8192]{0:T(1024)} %broadcast_clamp_fusion.2) | copy-start | bytes 98308
  403.2 9.0 %copy-start.1 = (f32[32,256,256]{2,1,0:T(8,128)}, f32[32,256,256]{2,1,0:T(8,128)S(1)}, u32[]{:S(2)}) copy-start(f32[32,256,256]{2,1,0:T(8,128)S(1)} %exponential_multiply_fusion) | copy-start | bytes 25165828
  640.1 15.6 %all-to-all-start.1 = ((f32[3,128,128]{2,0,1:T(4,128)}), f32[3,128,128]{2,0,1:T(4,128)S(1)}, u32[]{:S(2)}, u32[]{:S(2)}) async-start(f32[3,128,128]{2,0,1:T(4,128)} %copy.145), calls=%async_computation.1 | async-start | bytes 524288 | tf_op jit(solution)/shard_map/all_to_all | solution.py:165
  655.7 97.6 %copy-start.2 = (f32[16,8192]{1,0:T(8,128)S(1)}, f32[16,8192]{1,0:T(8,128)}, u32[]{:S(2)}) copy-start(f32[16,8192]{1,0:T(8,128)} %stack.25) | copy-start | bytes 1572868
where the time goes:
time: 766 us; the launch traced here: 755 us
  other arithmetic  320 us (42%)
  local copies, waits for them, and re-layouts  253 us (33%)
  matrix products  120 us (16%)
  waiting for transfers between devices  42.9 us (6%)
  starting transfers between devices  16.5 us (2%)
    scatter-add x1, other arithmetic, per_device(): jnp.zeros((slot_total, 3), jnp.float32).at[tile_slots.reshape(-1)]  178 us
    gather x8, local copies, waits for them, and re-layouts, render_block(): picked = jnp.moveaxis(attr_rows[slot_ids], 2, 0)  137 us
    scatter-add x1, other arithmetic, per_device(): jnp.zeros((owned, 3), jnp.float32).at[flat_ids].add(jnp.transpose(returned))  89.8 us
    dot_general x4, matrix products, render_block(): jnp.einsum('npg,gh->nph', log_keep, strictly_before, precision=lax.Precis...  64.1 us
    gather x1, local copies, waits for them, and re-layouts, per_device(): chosen_rows = jnp.transpose(jnp.transpose(gaussians)[flat_ids])  56.9 us
    all_to_all x1, waiting for transfers between devices, send_ahead(): lax.all_to_all(buffer, ('cell', 'tile'), split_axis=1, concat_axis=1, til...  42.7 us
    dot_general x4, matrix products, render_block(): jnp.einsum('npg,cng->cnp', weight, picked[6:9], precision=lax.Precision.H...  34.8 us
    reduce_sum x2, other arithmetic, render_block(): return (log_trans + jnp.sum(log_keep, axis=2), colour_part, colour_grad)  25 us
  transfers between devices with their start and end apart: 2, of which 2 were waited for; matrix products, arithmetic and copies ran while one was open for 3% of the time, Pallas kernels for 0%

commit v1 on v0

v1 whole, which is shorter than its diff:
```python
import jax
import jax.numpy as jnp
from jax import lax
from jax.experimental import pallas as pl
from jax.experimental.pallas import tpu as pltpu
from jax.sharding import PartitionSpec as P

AXES = ("cell", "tile")
PEERS = 128
WIDTH = 128
OWNED = 8192
SLOTS = 16384
TILE_DEV = 32
BLOCKS = 4
PARAMS = 59
ATTRS = 9
UNIT = 256
Q_OWN = OWNED // UNIT
Q_SLOT = SLOTS // UNIT
LANES = 128
PAD_PARAMS = 64
F32 = jnp.float32
BF16 = jnp.bfloat16
VMEM_BYTES = 48 * 2**20

FOCAL_LENGTH = 256.0
CENTRE_SHIFT = 128.0
BLUR_TERM = 0.3
LOG2E = 1.4426950408889634
HARM_ZERO = 0.28209479177387814
HARM_ONE = 0.4886025119029199
HARM_TWO = (
    1.0925484305920792,
    -1.0925484305920792,
    0.31539156525252005,
    -1.0925484305920792,
    0.5462742152960396,
)
HARM_THREE = (
    -0.5900435899266435,
    2.890611442640554,
    -0.4570457994644658,
    0.3731763325901154,
    -0.4570457994644658,
    1.445305721320277,
    -0.5900435899266435,
)


def sh_basis(mean_x, mean_y, mean_z):
    inverse_norm = 1.0 / jnp.sqrt(mean_x * mean_x + mean_y * mean_y + mean_z * mean_z)
    unit_x = mean_x * inverse_norm
    unit_y = mean_y * inverse_norm
    unit_z = mean_z * inverse_norm
    square_x = unit_x * unit_x
    square_y = unit_y * unit_y
    square_z = unit_z * unit_z
    return [
        HARM_ZERO * jnp.ones_like(unit_x),
        -HARM_ONE * unit_y,
        HARM_ONE * unit_z,
        -HARM_ONE * unit_x,
        HARM_TWO[0] * unit_x * unit_y,
        HARM_TWO[1] * unit_y * unit_z,
        HARM_TWO[2] * (2.0 * square_z - square_x - square_y),
        HARM_TWO[3] * unit_x * unit_z,
        HARM_TWO[4] * (square_x - square_y),
        HARM_THREE[0] * unit_y * (3.0 * square_x - square_y),
        HARM_THREE[1] * unit_x * unit_y * unit_z,
        HARM_THREE[2] * unit_y * (4.0 * square_z - square_x - square_y),
        HARM_THREE[3] * unit_z * (2.0 * square_z - 3.0 * square_x - 3.0 * square_y),
        HARM_THREE[4] * unit_x * (4.0 * square_z - square_x - square_y),
        HARM_THREE[5] * unit_z * (square_x - square_y),
        HARM_THREE[6] * unit_x * (square_x - 3.0 * square_y),
    ]


def project(param):
    mean_x, mean_y, mean_z = param(0), param(1), param(2)
    scales = [jnp.exp(param(3 + axis)) for axis in range(3)]
    quat = [param(6 + part) for part in range(4)]
    quat_norm = jnp.sqrt(quat[0] * quat[0] + quat[1] * quat[1] + quat[2] * quat[2] + quat[3] * quat[3])
    quat_w, quat_x, quat_y, quat_z = (part / quat_norm for part in quat)
    rotation = [
        [
            1.0 - 2.0 * (quat_y * quat_y + quat_z * quat_z),
            2.0 * (quat_x * quat_y - quat_w * quat_z),
            2.0 * (quat_x * quat_z + quat_w * quat_y),
        ],
        [
            2.0 * (quat_x * quat_y + quat_w * quat_z),
            1.0 - 2.0 * (quat_x * quat_x + quat_z * quat_z),
            2.0 * (quat_y * quat_z - quat_w * quat_x),
        ],
        [
            2.0 * (quat_x * quat_z - quat_w * quat_y),
            2.0 * (quat_y * quat_z + quat_w * quat_x),
            1.0 - 2.0 * (quat_x * quat_x + quat_y * quat_y),
        ],
    ]
    scaled = [[rotation[row][col] * scales[col] for col in range(3)] for row in range(3)]
    sigma = [
        [sum(scaled[row][inner] * scaled[col][inner] for inner in range(3)) for col in range(3)]
        for row in range(3)
    ]
    inverse_depth = 1.0 / mean_z
    jac_diag = FOCAL_LENGTH * inverse_depth
    jac_first = -FOCAL_LENGTH * mean_x * inverse_depth * inverse_depth
    jac_second = -FOCAL_LENGTH * mean_y * inverse_depth * inverse_depth
    upper_row = [jac_diag * sigma[0][col] + jac_first * sigma[2][col] for col in range(3)]
    lower_row = [jac_diag * sigma[1][col] + jac_second * sigma[2][col] for col in range(3)]
    entry_a = upper_row[0] * jac_diag + upper_row[2] * jac_first + BLUR_TERM
    entry_b = upper_row[1] * jac_diag + upper_row[2] * jac_second
    entry_c = lower_row[1] * jac_diag + lower_row[2] * jac_second + BLUR_TERM
    determinant = entry_a * entry_c - entry_b * entry_b
    centre_u = FOCAL_LENGTH * mean_x * inverse_depth + CENTRE_SHIFT
    centre_v = FOCAL_LENGTH * mean_y * inverse_depth + CENTRE_SHIFT
    log_opacity = jnp.maximum(-jnp.log2(1.0 + jnp.exp(-param(10))), -10000.0)
    basis = sh_basis(mean_x, mean_y, mean_z)
    colour = [0.5 + sum(param(11 + 16 * c + k) * basis[k] for k in range(16)) for c in range(3)]
    attributes = [
        colour[0],
        colour[1],
        centre_u,
        centre_v,
        entry_c / determinant,
        -entry_b / determinant,
        entry_a / determinant,
        log_opacity,
        colour[2],
    ]
    kept = [jnp.where(value == value, jnp.clip(value, -1e30, 1e30), 0.0) for value in attributes]
    return kept, basis


def split_three(values):
    high = values.astype(BF16)
    rest = values - high.astype(F32)
    middle = rest.astype(BF16)
    low = (rest - middle.astype(F32)).astype(BF16)
    return high, middle, low


def split_two(values):
    high = values.astype(BF16)
    return high, (values - high.astype(F32)).astype(BF16)


def build_table(rows_ref, table_ref, ninth_ref, groups):
    for pair in range(groups // 2):
        part = []
        for q in (2 * pair, 2 * pair + 1):
            part.append(
                jnp.concatenate(
                    [rows_ref[pl.ds(18 * q, 8), :], rows_ref[pl.ds(18 * q + 9, 8), :]], axis=1
                )
            )
        pieces = split_three(jnp.concatenate(part, axis=0))
        for index, piece in enumerate(pieces):
            table_ref[pl.ds(16 * pair, 16), pl.ds(UNIT * index, UNIT)] = piece
    ninth = jnp.concatenate(
        [rows_ref[pl.ds(8, groups, stride=18), :], rows_ref[pl.ds(17, groups, stride=18), :]], axis=1
    )
    for index, piece in enumerate(split_two(ninth)):
        ninth_ref[:, pl.ds(UNIT * index, UNIT)] = piece


def one_hot(low_index):
    rows = lax.broadcasted_iota(jnp.int32, (UNIT, UNIT), 0)
    return jnp.where(rows == low_index, 1.0, 0.0).astype(BF16)


def gather_block(entries, table_ref, ninth_ref, groups):
    low_index = entries & (UNIT - 1)
    high_index = entries >> 8
    chosen = one_hot(low_index)
    tripled = jnp.concatenate([chosen, chosen, chosen], axis=0)
    every = jnp.dot(table_ref[...], tripled, preferred_element_type=F32)
    high_rows = jnp.broadcast_to(high_index, (8, UNIT))
    picked = jnp.zeros((8, UNIT), F32)
    for q in range(groups):
        picked = jnp.where(high_rows == q, every[8 * q : 8 * q + 8], picked)
    every_ninth = jnp.dot(ninth_ref[...], tripled[: 2 * UNIT], preferred_element_type=F32)
    group_rows = lax.broadcasted_iota(jnp.int32, (groups, UNIT), 0)
    ninth = jnp.sum(jnp.where(group_rows == high_index, every_ninth, 0.0), axis=0, keepdims=True)
    return picked, ninth


def scatter_terms(entries, values, groups):
    low_index = entries & (UNIT - 1)
    high_index = entries >> 8
    chosen = one_hot(low_index)
    group_rows = lax.broadcasted_iota(jnp.int32, (groups, UNIT), 0)
    member = group_rows == high_index
    highs, lows = [], []
    for c in range(3):
        value = jnp.where(member, values[c : c + 1], 0.0)
        high, low = split_two(value)
        highs.append(high)
        lows.append(low)
    left = jnp.concatenate([jnp.concatenate(highs, axis=0), jnp.concatenate(lows, axis=0)], axis=1)
    return left, jnp.concatenate([chosen, chosen], axis=1)


def dot_transposed(left, right):
    return lax.dot_general(left, right, (((1,), (1,)), ((), ())), preferred_element_type=F32)


OWN_UNROLL = 8


def own_kernel(gaussians, index_ref, send_ref, basis_ref, params, rows_ref, table_ref, ninth_ref, sems):
    def fetch(k):
        return pltpu.make_async_copy(
            gaussians.at[:, pl.ds(pl.multiple_of(k * LANES, LANES), LANES)],
            params.at[pl.ds(pl.multiple_of(k * PAD_PARAMS, PAD_PARAMS), PARAMS), :],
            sems.at[k],
        )

    def start(k, carry):
        fetch(k).start()
        return carry

    lax.fori_loop(0, OWNED // LANES, start, 0)

    def group(kb, carry):
        for k in range(8):
            fetch(8 * kb + k).wait()

        def param(a):
            return params[pl.ds(kb * 8 * PAD_PARAMS + a, 8, stride=PAD_PARAMS), :]

        attributes, basis = project(param)
        for a in range(ATTRS):
            rows_ref[pl.ds(kb * 8 * ATTRS + a, 8, stride=ATTRS), :] = attributes[a]
        for k in range(16):
            basis_ref[pl.ds(kb * 8 * 16 + k, 8, stride=16), :] = basis[k]
        return carry

    lax.fori_loop(0, OWNED // LANES // 8, group, 0)
    build_table(rows_ref, table_ref, ninth_ref, Q_OWN)

    def blocks(i, carry):
        index_rows = index_ref[pl.ds(pl.multiple_of(2 * OWN_UNROLL * i, 8), 2 * OWN_UNROLL), :]
        for j in range(OWN_UNROLL):
            entries = jnp.concatenate([index_rows[2 * j : 2 * j + 1], index_rows[2 * j + 1 : 2 * j + 2]], axis=1)
            picked, ninth = gather_block(entries, table_ref, ninth_ref, Q_OWN)
            for half in range(2):
                row = pl.multiple_of(i * (18 * OWN_UNROLL), 8) + 18 * j + 9 * half
                lanes = slice(LANES * half, LANES * half + LANES)
                send_ref[pl.ds(row, 8), :] = picked[:, lanes]
                send_ref[pl.ds(row + 8, 1), :] = ninth[:, lanes]
        return carry

    lax.fori_loop(0, PEERS // 2 // OWN_UNROLL, blocks, 0)


GATHER_UNROLL = 4
RENDER_UNROLL = 2
SCATTER_UNROLL = 4
MOST = TILE_DEV * BLOCKS
LISTED = MOST + 8


def render_kernel(
    received,
    slots_ref,
    cot_ref,
    counts_ref,
    rank_ref,
    image_ref,
    grad_ref,
    table_ref,
    ninth_ref,
    triangle_ref,
    entries_ref,
    attr_ref,
    attr_ninth_ref,
    value_ref,
    total_ref,
    picture_ref,
    listed,
):
    build_table(received, table_ref, ninth_ref, Q_SLOT)
    before = lax.broadcasted_iota(jnp.int32, (UNIT, UNIT), 0)
    after = lax.broadcasted_iota(jnp.int32, (UNIT, UNIT), 1)
    triangle = jnp.where(before < after, 1.0, 0.0).astype(BF16)
    triangle_ref[pl.ds(0, UNIT), :] = triangle
    triangle_ref[pl.ds(UNIT, UNIT), :] = triangle
    picture_ref[...] = jnp.zeros_like(picture_ref)
    total_ref[...] = jnp.zeros_like(total_ref)

    def list_tile(t, n):
        count = counts_ref[t]

        def list_block(b, n):
            listed[n] = t * 8 + b
            entries_ref[n] = slots_ref[t, pl.ds(b, 1), :]
            return n + 1

        return lax.fori_loop(0, count, list_block, n)

    live = lax.fori_loop(0, TILE_DEV, list_tile, 0)
    for extra in range(8):
        listed[live + extra] = TILE_DEV * 8
        entries_ref[live + extra] = jnp.zeros((1, UNIT), jnp.int32)

    def gather_step(i, carry):
        for j in range(GATHER_UNROLL):
            n = i * GATHER_UNROLL + j
            picked, ninth = gather_block(entries_ref[n], table_ref, ninth_ref, Q_SLOT)
            attr_ref[n] = picked
            attr_ninth_ref[n] = ninth
        return carry

    lax.fori_loop(0, (live + GATHER_UNROLL - 1) // GATHER_UNROLL, gather_step, 0)

    rank = rank_ref[0]
    lane_ones = jnp.ones((1, UNIT), F32)
    lane_zeros = jnp.zeros((4, UNIT), F32)
    across = lax.broadcasted_iota(jnp.int32, (8, UNIT), 0)

    def render_one(n, trans):
        code = listed[n]
        t = code >> 3
        first = (code & 7) == 0
        local_tile = (rank * TILE_DEV + t) % 256
        origin_x = (16 * (local_tile % 16)).astype(F32) + 0.5
        origin_y = (16 * (local_tile // 16)).astype(F32) + 0.5
        picked = attr_ref[n]

        def wide(row):
            return jnp.broadcast_to(picked[row : row + 1], (8, UNIT))

        centre_u, centre_v = wide(2), wide(3)
        form_a = wide(4) * (-0.5 * LOG2E)
        form_b = wide(5) * (-LOG2E)
        form_c = wide(6) * (-0.5 * LOG2E)
        log_opacity = wide(7)
        constant, linear = [], []
        for half in range(2):
            delta_x = (across.astype(F32) + (origin_x + 8.0 * half)) - centre_u
            constant.append(form_a * delta_x * delta_x + log_opacity)
            linear.append(form_b * delta_x)
        powers = []
        for y in range(16):
            delta_y = (origin_y + y) - centre_v
            bent = form_c * delta_y
            for half in range(2):
                powers.append(constant[half] + delta_y * (linear[half] + bent))
        alpha = jnp.exp2(jnp.concatenate(powers, axis=0))
        log_keep = jnp.log2(1.0 - alpha)
        kept_high, kept_low = split_two(log_keep)
        earlier = jnp.dot(
            jnp.concatenate([kept_high, kept_low], axis=1), triangle_ref[...], preferred_element_type=F32
        )
        weight = alpha * jnp.exp2(earlier)
        weight_high, weight_low = split_two(weight)
        columns = jnp.concatenate([picked[0:2], attr_ninth_ref[n], lane_ones, lane_zeros], axis=0)
        colour_high, colour_low = split_two(columns)
        nothing = jnp.zeros((8, UNIT), BF16)
        left = jnp.concatenate(
            [
                jnp.concatenate([colour_high, colour_low], axis=0),
                jnp.concatenate([colour_high, nothing], axis=0),
            ],
            axis=1,
        )
        seen = dot_transposed(left, jnp.concatenate([weight_high, weight_low], axis=1))
        seen = seen[:8] + seen[8:]
        trans = jnp.where(first, jnp.ones_like(trans), trans)
        shown = seen * trans
        cot = jnp.concatenate([cot_ref[0, pl.ds(jnp.minimum(t, TILE_DEV - 1), 1), :],
                               cot_ref[1, pl.ds(jnp.minimum(t, TILE_DEV - 1), 1), :],
                               cot_ref[2, pl.ds(jnp.minimum(t, TILE_DEV - 1), 1), :],
                               lane_ones, lane_zeros], axis=0)
        cot_high, cot_low = split_two(cot * trans)
        left = jnp.concatenate(
            [
                jnp.concatenate([cot_high, cot_low], axis=0),
                jnp.concatenate([cot_high, nothing], axis=0),
            ],
            axis=1,
        )
        back = jnp.dot(
            left, jnp.concatenate([weight_high, weight_low], axis=0), preferred_element_type=F32
        )
        back = back[:8] + back[8:]
        value_ref[n] = jnp.where(t < TILE_DEV, back, 0.0)
        picture_ref[t] = jnp.where(first, shown, picture_ref[t] + shown)
        return jnp.maximum(trans * (1.0 - seen[3:4]), 0.0)

    def render_step(i, trans):
        for j in range(RENDER_UNROLL):
            trans = render_one(i * RENDER_UNROLL + j, trans)
        return trans

    lax.fori_loop(0, (live + RENDER_UNROLL - 1) // RENDER_UNROLL, render_step, jnp.ones((1, UNIT), F32))
    for extra in range(8):
        value_ref[live + extra] = jnp.zeros((8, UNIT), F32)

    def scatter_step(i, carry):
        lefts, rights = [], []
        for j in range(SCATTER_UNROLL):
            n = i * SCATTER_UNROLL + j
            left, right = scatter_terms(entries_ref[n], value_ref[n], Q_SLOT)
            lefts.append(left)
            rights.append(right)
        total_ref[...] += dot_transposed(jnp.concatenate(lefts, axis=1), jnp.concatenate(rights, axis=1))
        return carry

    lax.fori_loop(0, (live + SCATTER_UNROLL - 1) // SCATTER_UNROLL, scatter_step, 0)
    for c in range(3):
        for half in range(2):
            grad_ref[pl.ds(3 * half + c, Q_SLOT, stride=6), :] = total_ref[
                pl.ds(c * Q_SLOT, Q_SLOT), pl.ds(half * LANES, LANES)
            ]
    for t in range(TILE_DEV):
        for c in range(3):
            image_ref[c, pl.ds(t, 1), :] = picture_ref[t, pl.ds(c, 1), :]


FINISH_UNROLL = 4


def finish_kernel(returned, index_ref, basis_ref, out_ref, total_ref):
    total_ref[...] = jnp.zeros_like(total_ref)

    def scatter_step(i, carry):
        rows = returned[pl.ds(pl.multiple_of(i * (6 * FINISH_UNROLL), 8), 6 * FINISH_UNROLL), :]
        index_rows = index_ref[pl.ds(pl.multiple_of(2 * FINISH_UNROLL * i, 8), 2 * FINISH_UNROLL), :]
        lefts, rights = [], []
        for j in range(FINISH_UNROLL):
            entries = jnp.concatenate([index_rows[2 * j : 2 * j + 1], index_rows[2 * j + 1 : 2 * j + 2]], axis=1)
            values = jnp.concatenate([rows[6 * j : 6 * j + 3], rows[6 * j + 3 : 6 * j + 6]], axis=1)
            left, right = scatter_terms(entries, values, Q_OWN)
            lefts.append(left)
            rights.append(right)
        total_ref[...] += dot_transposed(jnp.concatenate(lefts, axis=1), jnp.concatenate(rights, axis=1))
        return carry

    lax.fori_loop(0, PEERS // 2 // FINISH_UNROLL, scatter_step, 0)
    for k in range(OWNED // LANES):
        basis = basis_ref[pl.ds(16 * k, 16), :]
        for c in range(3):
            grad = total_ref[pl.ds(c * Q_OWN + k // 2, 1), pl.ds((k % 2) * LANES, LANES)]
            out_ref[pl.ds(16 * c, 16), pl.ds(k * LANES, LANES)] = basis * grad


def exchange(buffer):
    return lax.all_to_all(buffer, AXES, split_axis=0, concat_axis=0, tiled=True)


def per_device(gaussians, send_index, tile_slots, block_count, cotangent):
    vmem = pl.BlockSpec(memory_space=pltpu.VMEM)
    smem = pl.BlockSpec(memory_space=pltpu.SMEM)
    limits = pltpu.CompilerParams(vmem_limit_bytes=VMEM_BYTES)
    shape = jax.ShapeDtypeStruct
    rank = lax.axis_index(AXES).astype(jnp.int32).reshape(1)
    index = send_index.reshape(PEERS, WIDTH)
    send, basis = pl.pallas_call(
        own_kernel,
        out_shape=(shape((ATTRS * PEERS, WIDTH), F32), shape((16 * OWNED // LANES, LANES), F32)),
        in_specs=[pl.BlockSpec(memory_space=pl.ANY), vmem],
        out_specs=(vmem, vmem),
        scratch_shapes=[
            pltpu.VMEM((PAD_PARAMS * OWNED // LANES, LANES), F32),
            pltpu.VMEM((ATTRS * OWNED // LANES, LANES), F32),
            pltpu.VMEM((8 * Q_OWN, 3 * UNIT), BF16),
            pltpu.VMEM((Q_OWN, 2 * UNIT), BF16),
            pltpu.SemaphoreType.DMA((OWNED // LANES,)),
        ],
        compiler_params=limits,
        name="project_and_pack",
    )(gaussians, index)
    received = exchange(send.reshape(PEERS, ATTRS * WIDTH)).reshape(ATTRS * PEERS, WIDTH)
    image, slot_grad = pl.pallas_call(
        render_kernel,
        out_shape=(shape((3, TILE_DEV, UNIT), F32), shape((3 * PEERS, WIDTH), F32)),
        in_specs=[vmem, vmem, vmem, smem, smem],
        out_specs=(vmem, vmem),
        scratch_shapes=[
            pltpu.VMEM((8 * Q_SLOT, 3 * UNIT), BF16),
            pltpu.VMEM((Q_SLOT, 2 * UNIT), BF16),
            pltpu.VMEM((2 * UNIT, UNIT), BF16),
            pltpu.VMEM((LISTED, 1, UNIT), jnp.int32),
            pltpu.VMEM((LISTED, 8, UNIT), F32),
            pltpu.VMEM((LISTED, 1, UNIT), F32),
            pltpu.VMEM((LISTED, 8, UNIT), F32),
            pltpu.VMEM((3 * Q_SLOT, UNIT), F32),
            pltpu.VMEM((TILE_DEV + 1, 8, UNIT), F32),
            pltpu.SMEM((LISTED,), jnp.int32),
        ],
        compiler_params=limits,
        name="render",
    )(received, tile_slots, cotangent, block_count, rank)
    returned = exchange(slot_grad.reshape(PEERS, 3 * WIDTH)).reshape(3 * PEERS, WIDTH)
    sh_grad = pl.pallas_call(
        finish_kernel,
        out_shape=shape((48, OWNED), F32),
        in_specs=[vmem, vmem, vmem],
        out_specs=vmem,
        scratch_shapes=[pltpu.VMEM((3 * Q_OWN, UNIT), F32)],
        compiler_params=limits,
        name="finish",
    )(returned, index, basis)
    return image, sh_grad


def solution(mesh):
    placed = (
        P(None, AXES),
        P(AXES, None, None),
        P(AXES, None, None),
        P(AXES),
        P(None, AXES, None),
    )
    return jax.shard_map(
        per_device,
        mesh=mesh,
        in_specs=placed,
        out_specs=(P(None, AXES, None), P(None, AXES)),
        check_vma=False,
    )
```

time: 766 us -> 147 us (0.19); the launches traced: 755 us -> 147 us
  other arithmetic: 320 us -> 0 us
  local copies, waits for them, and re-layouts: 253 us -> 2.44 us
  matrix products: 120 us -> 0 us
  blocking collectives: 0 us -> 65.5 us
  Pallas kernels: 0 us -> 52.4 us
  waiting for transfers between devices: 42.9 us -> 14 us
    scatter-add x2 -> x0, other arithmetic: 268 us -> none  [the longest x1 178 us: per_device(): jnp.zeros((slot_total, 3), jnp.float32).at[tile_slots.reshape(-1)]]
    gather x9 -> x0, local copies, waits for them, and re-layouts: 194 us -> none  [the longest x8 137 us: render_block(): picked = jnp.moveaxis(attr_rows[slot_ids], 2, 0)]
    dot_general x12 -> x0, matrix products: 120 us -> none  [the longest x4 64.1 us: render_block(): jnp.einsum('npg,gh->nph', log_keep, strictly_before, precision=lax.Precis...]
    all_to_all x0 -> x1, blocking collectives: none -> 65.5 us  [exchange(): return lax.all_to_all(buffer, AXES, split_axis=0, concat_axis=0, tiled=True)]
    pallas_call x0 -> x3, Pallas kernels: none -> 52.4 us  [the longest x1 29.5 us: per_device(): pl.pallas_call(render_kernel, out_shape=(shape((3, TILE_DEV, UNIT), F32),...]
    all_to_all x2 -> x1, waiting for transfers between devices: 42.9 us -> 14 us  [exchange(): return lax.all_to_all(buffer, AXES, split_axis=0, concat_axis=0, tiled=True)]
    reduce_sum x4 -> x0, other arithmetic: 28.3 us -> none  [the longest x2 25 us: render_block(): return (log_trans + jnp.sum(log_keep, axis=2), colour_part, colour_grad)]
    transpose x3 -> x0, local copies, waits for them, and re-layouts: 16.4 us -> none  [the longest x1 8.57 us: per_device(): entry_rows = jnp.transpose(entry_grad.reshape(3, -1))]
  transfers between devices with their start and end apart: 2 -> 1, of which waited for: 2 -> 1; matrix products, arithmetic and copies ran while one was open for 3% -> 0% of each run, Pallas kernels for 0% -> 0%
where the time goes in v1:
time: 147 us
  blocking collectives  65.5 us (45%)
  Pallas kernels  52.4 us (36%)
  waiting for transfers between devices  14 us (10%)
  starting transfers between devices  11.5 us (8%)
  local copies, waits for them, and re-layouts  2.44 us (2%)
    all_to_all x1, blocking collectives, exchange(): return lax.all_to_all(buffer, AXES, split_axis=0, concat_axis=0, tiled=True)  65.5 us
    pallas_call x1, Pallas kernels, per_device(): pl.pallas_call(render_kernel, out_shape=(shape((3, TILE_DEV, UNIT), F32),...  29.5 us
    all_to_all x1, waiting for transfers between devices, exchange(): return lax.all_to_all(buffer, AXES, split_axis=0, concat_axis=0, tiled=True)  14 us
    pallas_call x1, Pallas kernels, per_device(): pl.pallas_call(own_kernel, out_shape=(shape((ATTRS * PEERS, WIDTH), F32),...  13.9 us
    all_to_all x1, starting transfers between devices, exchange(): return lax.all_to_all(buffer, AXES, split_axis=0, concat_axis=0, tiled=True)  11.5 us
    pallas_call x1, Pallas kernels, per_device(): pl.pallas_call(finish_kernel, out_shape=shape((48, OWNED), F32), in_specs...  9.01 us
  transfers between devices with their start and end apart: 1, of which 1 were waited for; matrix products, arithmetic and copies ran while one was open for 0% of the time, Pallas kernels for 0%

profile of v1, /device:TPU:1, one launch (start us, length us, event | category | flops | bytes accessed | tf_op | source)
XLA Modules:
  0.0 146.6 jit_solution(13409681343833735964)
XLA Ops:
  0.6 0.0 copy-start.5
  0.6 0.0 copy-start
  0.7 1.6 %copy-done = f32[59,8192]{1,0:T(8,128)S(1)} copy-done((f32[59,8192]{1,0:T(8,128)S(1)}, f32[59,8192]{1,0:T(8,128)}, u32[]{:S(2)}) %copy-start) | copy-done | bytes 1933336
  2.2 0.0 copy-start.1
  2.2 0.8 copy-done.1
  3.1 0.0 copy-start.3
  3.1 0.0 copy-start.4
  3.1 0.0 copy-start.2
  3.1 13.9 %project_and_pack.1 = (f32[1152,128]{1,0:T(8,128)}, f32[1024,128]{1,0:T(8,128)S(1)}) custom-call(f32[59,8192]{1,0:T(8,128)S(1)} %copy-done, s32[128,128]{1,0:T(8,128)S(1)} %bitcast.8), custom_call_target="tpu_custom_call" | custom-call | tf_op jit(solution)/shard_map/project_and_pack/pallas_call | solution.py:461
  17.0 11.5 %all-to-all-start = ((f32[128,1,1152]{2,1,0:T(1,128)}), f32[128,1,1152]{2,1,0:T(1,128)S(1)}, u32[]{:S(2)}, u32[]{:S(2)}) async-start(f32[128,1,1152]{2,1,0:T(1,128)} %bitcast.1), calls=%async_computation | async-start | bytes 1179648 | tf_op jit(solution)/shard_map/all_to_all | solution.py:451
  28.5 14.0 %all-to-all-done = f32[128,1,1152]{2,1,0:T(1,128)S(1)} async-done(((f32[128,1,1152]{2,1,0:T(1,128)}), f32[128,1,1152]{2,1,0:T(1,128)S(1)}, u32[]{:S(2)}, u32[]{:S(2)}) %all-to-all-start) | async-done | bytes 589856 | tf_op jit(solution)/shard_map/all_to_all | solution.py:451
  42.5 0.0 copy-done.5
  42.5 0.0 copy-done.3
  42.5 0.0 copy-done.4
  42.5 29.5 %render.1 = (f32[3,32,256]{2,1,0:T(8,128)}, f32[384,128]{1,0:T(8,128)S(1)}) custom-call(f32[1152,128]{1,0:T(8,128)S(1)} %bitcast.6, s32[32,4,256]{2,1,0:T(4,128)S(1)} %copy-done.3, f32[3,32,256]{2,1,0:T(8,128)S(1)} %copy-done.4, s32[32]{0:T(128)S(1)} %copy-done.5, s32[1]{0:T(128)} %bitcast.3.rank_ref), custom_call_target="tpu_custom_call" | custom-call | tf_op jit(solution)/shard_map/render/pallas_call | solution.py:477
  72.0 65.5 %all_to_all.18 = f32[128,1,384]{2,1,0:T(1,128)S(1)} all-to-all(f32[128,1,384]{2,1,0:T(1,128)S(1)} %bitcast.10), channel_id=1, replica_groups=mesh['cell'=8,'tile'=16] {'cell','tile'}, dimensions={0} | all-to-all | bytes 393216 | tf_op jit(solution)/shard_map/all_to_all | solution.py:451
  137.5 0.0 copy-done.2
  137.5 9.0 %finish.1 = f32[48,8192]{1,0:T(8,128)} custom-call(f32[384,128]{1,0:T(8,128)S(1)} %bitcast.7, s32[128,128]{1,0:T(8,128)S(1)} %bitcast.9, f32[1024,128]{1,0:T(8,128)S(1)} %get-tuple-element.9.basis_ref), custom_call_target="tpu_custom_call" | custom-call | tf_op jit(solution)/shard_map/finish/pallas_call | solution.py:498
Async XLA Ops:
  0.6 41.9 %copy-start.5 = (s32[32]{0:T(128)S(1)}, s32[32]{0:T(128)}, u32[]{:S(2)}) copy-start(s32[32]{0:T(128)} %counts_ref.1) | copy-start | bytes 388
  0.6 1.6 %copy-start = (f32[59,8192]{1,0:T(8,128)S(1)}, f32[59,8192]{1,0:T(8,128)}, u32[]{:S(2)}) copy-start(f32[59,8192]{1,0:T(8,128)} %gaussians.1) | copy-start | bytes 5799940
  2.2 0.8 copy-start.1
  3.1 39.5 %copy-start.3 = (s32[32,4,256]{2,1,0:T(4,128)S(1)}, s32[32,4,256]{2,1,0:T(4,128)}, u32[]{:S(2)}) copy-start(s32[32,4,256]{2,1,0:T(4,128)} %slots_ref.1) | copy-start | bytes 393220
  3.1 39.5 %copy-start.4 = (f32[3,32,256]{2,1,0:T(8,128)S(1)}, f32[3,32,256]{2,1,0:T(8,128)}, u32[]{:S(2)}) copy-start(f32[3,32,256]{2,1,0:T(8,128)} %cot_ref.1) | copy-start | bytes 294916
  3.1 134.5 %copy-start.2 = (s32[1,128,128]{2,1,0:T(8,128)S(1)}, s32[1,128,128]{2,1,0:T(8,128)}, u32[]{:S(2)}) copy-start(s32[1,128,128]{2,1,0:T(8,128)} %param.6) | copy-start | bytes 196612
  17.0 25.5 %all-to-all-start = ((f32[128,1,1152]{2,1,0:T(1,128)}), f32[128,1,1152]{2,1,0:T(1,128)S(1)}, u32[]{:S(2)}, u32[]{:S(2)}) async-start(f32[128,1,1152]{2,1,0:T(1,128)} %bitcast.1), calls=%async_computation | async-start | bytes 1179648 | tf_op jit(solution)/shard_map/all_to_all | solution.py:451

commit v2 on v1

--- a/solution.py
+++ b/solution.py
@@ -146,23 +146,22 @@
     return high, (values - high.astype(F32)).astype(BF16)
 
 
-def build_table(rows_ref, table_ref, ninth_ref, groups):
+def build_table(rows_ref, table_ref, groups):
+    inner = lax.broadcasted_iota(jnp.int32, (16, UNIT), 0) & 7
     for pair in range(groups // 2):
-        part = []
+        part, ninth = [], []
         for q in (2 * pair, 2 * pair + 1):
-            part.append(
-                jnp.concatenate(
-                    [rows_ref[pl.ds(18 * q, 8), :], rows_ref[pl.ds(18 * q + 9, 8), :]], axis=1
-                )
-            )
-        pieces = split_three(jnp.concatenate(part, axis=0))
-        for index, piece in enumerate(pieces):
-            table_ref[pl.ds(16 * pair, 16), pl.ds(UNIT * index, UNIT)] = piece
-    ninth = jnp.concatenate(
-        [rows_ref[pl.ds(8, groups, stride=18), :], rows_ref[pl.ds(17, groups, stride=18), :]], axis=1
-    )
-    for index, piece in enumerate(split_two(ninth)):
-        ninth_ref[:, pl.ds(UNIT * index, UNIT)] = piece
+            halves = [rows_ref[pl.ds(18 * q, 8), :], rows_ref[pl.ds(18 * q + 9, 8), :]]
+            part.append(jnp.concatenate(halves, axis=1))
+            halves = [rows_ref[pl.ds(18 * q + 8, 1), :], rows_ref[pl.ds(18 * q + 17, 1), :]]
+            ninth.append(jnp.broadcast_to(jnp.concatenate(halves, axis=1), (8, UNIT)))
+        first, second, third = split_three(jnp.concatenate(part, axis=0))
+        high, low = split_two(jnp.concatenate(ninth, axis=0))
+        tail = jnp.where(
+            inner == 0, high.astype(F32), jnp.where(inner == 1, low.astype(F32), third.astype(F32))
+        ).astype(BF16)
+        for index, piece in enumerate((first, second, tail)):
+            table_ref[pl.ds(8 * groups * index + 16 * pair, 16), :] = piece
 
 
 def one_hot(low_index):
@@ -170,46 +169,37 @@
     return jnp.where(rows == low_index, 1.0, 0.0).astype(BF16)
 
 
-def gather_block(entries, table_ref, ninth_ref, groups):
-    low_index = entries & (UNIT - 1)
-    high_index = entries >> 8
-    chosen = one_hot(low_index)
-    tripled = jnp.concatenate([chosen, chosen, chosen], axis=0)
-    every = jnp.dot(table_ref[...], tripled, preferred_element_type=F32)
-    high_rows = jnp.broadcast_to(high_index, (8, UNIT))
-    picked = jnp.zeros((8, UNIT), F32)
+def gather_block(entries, table_ref, groups):
+    every = jnp.dot(table_ref[...], one_hot(entries & (UNIT - 1)), preferred_element_type=F32)
+    high_rows = jnp.broadcast_to(entries >> 8, (8, UNIT))
+    picked = [jnp.zeros((8, UNIT), F32)] * 3
     for q in range(groups):
-        picked = jnp.where(high_rows == q, every[8 * q : 8 * q + 8], picked)
-    every_ninth = jnp.dot(ninth_ref[...], tripled[: 2 * UNIT], preferred_element_type=F32)
+        member = high_rows == q
+        for index in range(3):
+            start = 8 * groups * index + 8 * q
+            picked[index] = jnp.where(member, every[start : start + 8], picked[index])
+    inner = lax.broadcasted_iota(jnp.int32, (8, UNIT), 0)
+    tail = picked[2]
+    return picked[0] + (picked[1] + jnp.where(inner < 2, 0.0, tail)), tail[0:1] + tail[1:2]
+
+
+def scatter_terms(entries, values, groups):
+    chosen = one_hot(entries & (UNIT - 1))
     group_rows = lax.broadcasted_iota(jnp.int32, (groups, UNIT), 0)
-    ninth = jnp.sum(jnp.where(group_rows == high_index, every_ninth, 0.0), axis=0, keepdims=True)
-    return picked, ninth
-
-
-def scatter_terms(entries, values, groups):
-    low_index = entries & (UNIT - 1)
-    high_index = entries >> 8
-    chosen = one_hot(low_index)
-    group_rows = lax.broadcasted_iota(jnp.int32, (groups, UNIT), 0)
-    member = group_rows == high_index
-    highs, lows = [], []
-    for c in range(3):
-        value = jnp.where(member, values[c : c + 1], 0.0)
-        high, low = split_two(value)
-        highs.append(high)
-        lows.append(low)
-    left = jnp.concatenate([jnp.concatenate(highs, axis=0), jnp.concatenate(lows, axis=0)], axis=1)
-    return left, jnp.concatenate([chosen, chosen], axis=1)
+    member = jnp.where(group_rows == (entries >> 8), 1.0, 0.0).astype(BF16)
+    high, low = split_two(values)
+    rows = [member * part[c : c + 1] for part in (high, low) for c in range(3)]
+    return jnp.concatenate(rows, axis=0), chosen
 
 
 def dot_transposed(left, right):
     return lax.dot_general(left, right, (((1,), (1,)), ((), ())), preferred_element_type=F32)
 
 
-OWN_UNROLL = 8
-
-
-def own_kernel(gaussians, index_ref, send_ref, basis_ref, params, rows_ref, table_ref, ninth_ref, sems):
+OWN_UNROLL = 32
+
+
+def own_kernel(gaussians, index_hbm, send_ref, basis_ref, params, rows_ref, table_ref, index_ref, sems, index_sem):
     def fetch(k):
         return pltpu.make_async_copy(
             gaussians.at[:, pl.ds(pl.multiple_of(k * LANES, LANES), LANES)],
@@ -222,6 +212,8 @@
         return carry
 
     lax.fori_loop(0, OWNED // LANES, start, 0)
+    index_copy = pltpu.make_async_copy(index_hbm, index_ref, index_sem)
+    index_copy.start()
 
     def group(kb, carry):
         for k in range(8):
@@ -238,13 +230,14 @@
         return carry
 
     lax.fori_loop(0, OWNED // LANES // 8, group, 0)
-    build_table(rows_ref, table_ref, ninth_ref, Q_OWN)
+    build_table(rows_ref, table_ref, Q_OWN)
+    index_copy.wait()
 
     def blocks(i, carry):
         index_rows = index_ref[pl.ds(pl.multiple_of(2 * OWN_UNROLL * i, 8), 2 * OWN_UNROLL), :]
         for j in range(OWN_UNROLL):
             entries = jnp.concatenate([index_rows[2 * j : 2 * j + 1], index_rows[2 * j + 1 : 2 * j + 2]], axis=1)
-            picked, ninth = gather_block(entries, table_ref, ninth_ref, Q_OWN)
+            picked, ninth = gather_block(entries, table_ref, Q_OWN)
             for half in range(2):
                 row = pl.multiple_of(i * (18 * OWN_UNROLL), 8) + 18 * j + 9 * half
                 lanes = slice(LANES * half, LANES * half + LANES)
@@ -255,9 +248,8 @@
     lax.fori_loop(0, PEERS // 2 // OWN_UNROLL, blocks, 0)
 
 
-GATHER_UNROLL = 4
-RENDER_UNROLL = 2
-SCATTER_UNROLL = 4
+GATHER_UNROLL = 8
+RENDER_UNROLL = 4
 MOST = TILE_DEV * BLOCKS
 LISTED = MOST + 8
 
@@ -271,22 +263,20 @@
     image_ref,
     grad_ref,
     table_ref,
-    ninth_ref,
     triangle_ref,
     entries_ref,
     attr_ref,
     attr_ninth_ref,
-    value_ref,
+    gone_ref,
     total_ref,
     picture_ref,
     listed,
 ):
-    build_table(received, table_ref, ninth_ref, Q_SLOT)
+    build_table(received, table_ref, Q_SLOT)
     before = lax.broadcasted_iota(jnp.int32, (UNIT, UNIT), 0)
     after = lax.broadcasted_iota(jnp.int32, (UNIT, UNIT), 1)
     triangle = jnp.where(before < after, 1.0, 0.0).astype(BF16)
-    triangle_ref[pl.ds(0, UNIT), :] = triangle
-    triangle_ref[pl.ds(UNIT, UNIT), :] = triangle
+    triangle_ref[...] = triangle
     picture_ref[...] = jnp.zeros_like(picture_ref)
     total_ref[...] = jnp.zeros_like(total_ref)
 
@@ -308,7 +298,7 @@
     def gather_step(i, carry):
         for j in range(GATHER_UNROLL):
             n = i * GATHER_UNROLL + j
-            picked, ninth = gather_block(entries_ref[n], table_ref, ninth_ref, Q_SLOT)
+            picked, ninth = gather_block(entries_ref[n], table_ref, Q_SLOT)
             attr_ref[n] = picked
             attr_ninth_ref[n] = ninth
         return carry
@@ -316,13 +306,13 @@
     lax.fori_loop(0, (live + GATHER_UNROLL - 1) // GATHER_UNROLL, gather_step, 0)
 
     rank = rank_ref[0]
-    lane_ones = jnp.ones((1, UNIT), F32)
-    lane_zeros = jnp.zeros((4, UNIT), F32)
-    across = lax.broadcasted_iota(jnp.int32, (8, UNIT), 0)
-
-    def render_one(n, trans):
+    lane_ones = jnp.zeros((5, UNIT), F32)
+    across = lax.broadcasted_iota(jnp.int32, (8, UNIT), 0).astype(F32)
+
+    def render_one(n):
         code = listed[n]
         t = code >> 3
+        source = jnp.minimum(t, TILE_DEV - 1)
         first = (code & 7) == 0
         local_tile = (rank * TILE_DEV + t) % 256
         origin_x = (16 * (local_tile % 16)).astype(F32) + 0.5
@@ -339,7 +329,7 @@
         log_opacity = wide(7)
         constant, linear = [], []
         for half in range(2):
-            delta_x = (across.astype(F32) + (origin_x + 8.0 * half)) - centre_u
+            delta_x = (across + (origin_x + 8.0 * half)) - centre_u
             constant.append(form_a * delta_x * delta_x + log_opacity)
             linear.append(form_b * delta_x)
         powers = []
@@ -350,13 +340,26 @@
                 powers.append(constant[half] + delta_y * (linear[half] + bent))
         alpha = jnp.exp2(jnp.concatenate(powers, axis=0))
         log_keep = jnp.log2(1.0 - alpha)
-        kept_high, kept_low = split_two(log_keep)
-        earlier = jnp.dot(
-            jnp.concatenate([kept_high, kept_low], axis=1), triangle_ref[...], preferred_element_type=F32
-        )
-        weight = alpha * jnp.exp2(earlier)
-        weight_high, weight_low = split_two(weight)
-        columns = jnp.concatenate([picked[0:2], attr_ninth_ref[n], lane_ones, lane_zeros], axis=0)
+        sums = jnp.dot(jnp.concatenate(split_two(log_keep), axis=0), triangle_ref[...], preferred_element_type=F32)
+        cot = jnp.concatenate([cot_ref[c, pl.ds(source, 1), :] for c in range(3)] + [lane_ones], axis=0)
+        cot_columns = jnp.transpose(cot)
+        kept = jnp.where(first, 0.0, 1.0)
+        back = [[jnp.zeros((8, LANES), F32) for half in range(2)] for c in range(3)]
+        weights = []
+        for p in range(UNIT // 8):
+            rows = slice(8 * p, 8 * p + 8)
+            gone = gone_ref[pl.ds(8 * p, 8), :] * kept
+            earlier = (sums[rows] + sums[UNIT + 8 * p : UNIT + 8 * p + 8]) + jnp.concatenate([gone, gone], axis=1)
+            weight = alpha[rows] * jnp.exp2(earlier)
+            last = (earlier + log_keep[rows])[:, UNIT - 1 : UNIT]
+            gone_ref[pl.ds(8 * p, 8), :] = jnp.broadcast_to(last, (8, LANES))
+            for c in range(3):
+                column = jnp.broadcast_to(cot_columns[rows, c : c + 1], (8, LANES))
+                for half in range(2):
+                    back[c][half] += column * weight[:, LANES * half : LANES * half + LANES]
+            weights.append(weight)
+        weight_high, weight_low = split_two(jnp.concatenate(weights, axis=0))
+        columns = jnp.concatenate([picked[0:2], attr_ninth_ref[n], lane_ones], axis=0)
         colour_high, colour_low = split_two(columns)
         nothing = jnp.zeros((8, UNIT), BF16)
         left = jnp.concatenate(
@@ -368,59 +371,43 @@
         )
         seen = dot_transposed(left, jnp.concatenate([weight_high, weight_low], axis=1))
         seen = seen[:8] + seen[8:]
-        trans = jnp.where(first, jnp.ones_like(trans), trans)
-        shown = seen * trans
-        cot = jnp.concatenate([cot_ref[0, pl.ds(jnp.minimum(t, TILE_DEV - 1), 1), :],
-                               cot_ref[1, pl.ds(jnp.minimum(t, TILE_DEV - 1), 1), :],
-                               cot_ref[2, pl.ds(jnp.minimum(t, TILE_DEV - 1), 1), :],
-                               lane_ones, lane_zeros], axis=0)
-        cot_high, cot_low = split_two(cot * trans)
-        left = jnp.concatenate(
-            [
-                jnp.concatenate([cot_high, cot_low], axis=0),
-                jnp.concatenate([cot_high, nothing], axis=0),
-            ],
-            axis=1,
-        )
-        back = jnp.dot(
-            left, jnp.concatenate([weight_high, weight_low], axis=0), preferred_element_type=F32
-        )
-        back = back[:8] + back[8:]
-        value_ref[n] = jnp.where(t < TILE_DEV, back, 0.0)
-        picture_ref[t] = jnp.where(first, shown, picture_ref[t] + shown)
-        return jnp.maximum(trans * (1.0 - seen[3:4]), 0.0)
-
-    def render_step(i, trans):
+        picture_ref[t] = jnp.where(first, seen, picture_ref[t] + seen)
+        sums_back = [
+            jnp.sum(jnp.concatenate(back[c], axis=1), axis=0, keepdims=True) for c in range(3)
+        ]
+        return jnp.where(t < TILE_DEV, jnp.concatenate(sums_back, axis=0), 0.0)
+
+    def scatter_pair(n, values):
+        lefts, rights = [], []
         for j in range(RENDER_UNROLL):
-            trans = render_one(i * RENDER_UNROLL + j, trans)
-        return trans
-
-    lax.fori_loop(0, (live + RENDER_UNROLL - 1) // RENDER_UNROLL, render_step, jnp.ones((1, UNIT), F32))
-    for extra in range(8):
-        value_ref[live + extra] = jnp.zeros((8, UNIT), F32)
-
-    def scatter_step(i, carry):
-        lefts, rights = [], []
-        for j in range(SCATTER_UNROLL):
-            n = i * SCATTER_UNROLL + j
-            left, right = scatter_terms(entries_ref[n], value_ref[n], Q_SLOT)
+            left, right = scatter_terms(entries_ref[n + j], values[j], Q_SLOT)
             lefts.append(left)
             rights.append(right)
         total_ref[...] += dot_transposed(jnp.concatenate(lefts, axis=1), jnp.concatenate(rights, axis=1))
-        return carry
-
-    lax.fori_loop(0, (live + SCATTER_UNROLL - 1) // SCATTER_UNROLL, scatter_step, 0)
+
+    def render_step(i, values):
+        n = i * RENDER_UNROLL
+        scatter_pair(jnp.maximum(n - RENDER_UNROLL, 0), values)
+        return tuple(render_one(n + j) for j in range(RENDER_UNROLL))
+
+    gone_ref[...] = jnp.zeros_like(gone_ref)
+    steps = (live + RENDER_UNROLL - 1) // RENDER_UNROLL
+    nothing_back = tuple(jnp.zeros((3, UNIT), F32) for j in range(RENDER_UNROLL))
+    values = lax.fori_loop(0, steps, render_step, nothing_back)
+    scatter_pair((steps - 1) * RENDER_UNROLL, values)
     for c in range(3):
         for half in range(2):
-            grad_ref[pl.ds(3 * half + c, Q_SLOT, stride=6), :] = total_ref[
-                pl.ds(c * Q_SLOT, Q_SLOT), pl.ds(half * LANES, LANES)
-            ]
+            lanes = pl.ds(half * LANES, LANES)
+            grad_ref[pl.ds(3 * half + c, Q_SLOT, stride=6), :] = (
+                total_ref[pl.ds(c * Q_SLOT, Q_SLOT), lanes]
+                + total_ref[pl.ds((3 + c) * Q_SLOT, Q_SLOT), lanes]
+            )
     for t in range(TILE_DEV):
         for c in range(3):
             image_ref[c, pl.ds(t, 1), :] = picture_ref[t, pl.ds(c, 1), :]
 
 
-FINISH_UNROLL = 4
+FINISH_UNROLL = 32
 
 
 def finish_kernel(returned, index_ref, basis_ref, out_ref, total_ref):
@@ -443,7 +430,11 @@
     for k in range(OWNED // LANES):
         basis = basis_ref[pl.ds(16 * k, 16), :]
         for c in range(3):
-            grad = total_ref[pl.ds(c * Q_OWN + k // 2, 1), pl.ds((k % 2) * LANES, LANES)]
+            lanes = pl.ds((k % 2) * LANES, LANES)
+            grad = (
+                total_ref[pl.ds(c * Q_OWN + k // 2, 1), lanes]
+                + total_ref[pl.ds((3 + c) * Q_OWN + k // 2, 1), lanes]
+            )
             out_ref[pl.ds(16 * c, 16), pl.ds(k * LANES, LANES)] = basis * grad
 
 
@@ -461,16 +452,17 @@
     send, basis = pl.pallas_call(
         own_kernel,
         out_shape=(shape((ATTRS * PEERS, WIDTH), F32), shape((16 * OWNED // LANES, LANES), F32)),
-        in_specs=[pl.BlockSpec(memory_space=pl.ANY), vmem],
+        in_specs=[pl.BlockSpec(memory_space=pltpu.HBM), pl.BlockSpec(memory_space=pltpu.HBM)],
         out_specs=(vmem, vmem),
         scratch_shapes=[
             pltpu.VMEM((PAD_PARAMS * OWNED // LANES, LANES), F32),
             pltpu.VMEM((ATTRS * OWNED // LANES, LANES), F32),
-            pltpu.VMEM((8 * Q_OWN, 3 * UNIT), BF16),
-            pltpu.VMEM((Q_OWN, 2 * UNIT), BF16),
+            pltpu.VMEM((24 * Q_OWN, UNIT), BF16),
+            pltpu.VMEM((PEERS, WIDTH), jnp.int32),
             pltpu.SemaphoreType.DMA((OWNED // LANES,)),
+            pltpu.SemaphoreType.DMA(()),
         ],
-        compiler_params=limits,
+        compiler_params=pltpu.CompilerParams(vmem_limit_bytes=62 * 2**20),
         name="project_and_pack",
     )(gaussians, index)
     received = exchange(send.reshape(PEERS, ATTRS * WIDTH)).reshape(ATTRS * PEERS, WIDTH)
@@ -480,14 +472,13 @@
         in_specs=[vmem, vmem, vmem, smem, smem],
         out_specs=(vmem, vmem),
         scratch_shapes=[
-            pltpu.VMEM((8 * Q_SLOT, 3 * UNIT), BF16),
-            pltpu.VMEM((Q_SLOT, 2 * UNIT), BF16),
-            pltpu.VMEM((2 * UNIT, UNIT), BF16),
+            pltpu.VMEM((24 * Q_SLOT, UNIT), BF16),
+            pltpu.VMEM((UNIT, UNIT), BF16),
             pltpu.VMEM((LISTED, 1, UNIT), jnp.int32),
             pltpu.VMEM((LISTED, 8, UNIT), F32),
             pltpu.VMEM((LISTED, 1, UNIT), F32),
-            pltpu.VMEM((LISTED, 8, UNIT), F32),
-            pltpu.VMEM((3 * Q_SLOT, UNIT), F32),
+            pltpu.VMEM((UNIT, LANES), F32),
+            pltpu.VMEM((6 * Q_SLOT, UNIT), F32),
             pltpu.VMEM((TILE_DEV + 1, 8, UNIT), F32),
             pltpu.SMEM((LISTED,), jnp.int32),
         ],
@@ -500,7 +491,7 @@
         out_shape=shape((48, OWNED), F32),
         in_specs=[vmem, vmem, vmem],
         out_specs=vmem,
-        scratch_shapes=[pltpu.VMEM((3 * Q_OWN, UNIT), F32)],
+        scratch_shapes=[pltpu.VMEM((6 * Q_OWN, UNIT), F32)],
         compiler_params=limits,
         name="finish",
     )(returned, index, basis)

time: 147 us -> 115 us (0.78)
  blocking collectives: 65.5 us -> 40.6 us
  Pallas kernels: 52.4 us -> 46.9 us
  local copies, waits for them, and re-layouts: 2.44 us -> 0.02 us
    all_to_all x1, blocking collectives: 65.5 us -> 40.6 us  [exchange(): return lax.all_to_all(buffer, AXES, split_axis=0, concat_axis=0, tiled=True)]
    pallas_call x1, Pallas kernels: 9.01 us -> 4.37 us  [per_device(): pl.pallas_call(finish_kernel, out_shape=shape((48, OWNED), F32), in_specs...]
    pallas_call x1, Pallas kernels: 13.9 us -> 10.9 us  [per_device(): pl.pallas_call(own_kernel, out_shape=(shape((ATTRS * PEERS, WIDTH), F32),...]
    unnamed x12 -> x10, local copies, waits for them, and re-layouts: 2.44 us -> 0.02 us
    pallas_call x1, Pallas kernels: 29.5 us -> 31.7 us  [per_device(): pl.pallas_call(render_kernel, out_shape=(shape((3, TILE_DEV, UNIT), F32),...]
where the time goes in v2:
time: 115 us; the launch traced here: 114 us
  Pallas kernels  46.9 us (41%)
  blocking collectives  40.6 us (35%)
  waiting for transfers between devices  14 us (12%)
  starting transfers between devices  11.5 us (10%)
    all_to_all x1, blocking collectives, exchange(): return lax.all_to_all(buffer, AXES, split_axis=0, concat_axis=0, tiled=True)  40.6 us
    pallas_call x1, Pallas kernels, per_device(): pl.pallas_call(render_kernel, out_shape=(shape((3, TILE_DEV, UNIT), F32),...  31.7 us
    all_to_all x1, waiting for transfers between devices, exchange(): return lax.all_to_all(buffer, AXES, split_axis=0, concat_axis=0, tiled=True)  14 us
    all_to_all x1, starting transfers between devices, exchange(): return lax.all_to_all(buffer, AXES, split_axis=0, concat_axis=0, tiled=True)  11.5 us
    pallas_call x1, Pallas kernels, per_device(): pl.pallas_call(own_kernel, out_shape=(shape((ATTRS * PEERS, WIDTH), F32),...  10.9 us
    pallas_call x1, Pallas kernels, per_device(): pl.pallas_call(finish_kernel, out_shape=shape((48, OWNED), F32), in_specs...  4.37 us
  transfers between devices with their start and end apart: 1, of which 1 were waited for; matrix products, arithmetic and copies ran while one was open for 0% of the time, Pallas kernels for 0%

profile of v2, /device:TPU:1, one launch (start us, length us, event | category | flops | bytes accessed | tf_op | source)
XLA Modules:
  0.0 113.7 jit_solution(13140811440110840233)
XLA Ops:
  0.6 0.0 copy-start.3
  0.6 0.0 copy-start.4
  0.7 0.0 copy-start.2
  0.7 0.0 copy-start.1
  0.7 10.9 %project_and_pack.1 = (f32[1152,128]{1,0:T(8,128)}, f32[1024,128]{1,0:T(8,128)}) custom-call(f32[59,8192]{1,0:T(8,128)} %gaussians.1, s32[128,128]{1,0:T(8,128)} %bitcast.8), custom_call_target="tpu_custom_call" | custom-call | tf_op jit(solution)/shard_map/project_and_pack/pallas_call | solution.py:452
  11.5 0.0 copy-start
  11.6 11.5 %all-to-all-start = ((f32[128,1,1152]{2,1,0:T(1,128)}), f32[128,1,1152]{2,1,0:T(1,128)S(1)}, u32[]{:S(2)}, u32[]{:S(2)}) async-start(f32[128,1,1152]{2,1,0:T(1,128)} %bitcast.11), calls=%async_computation | async-start | bytes 1179648 | tf_op jit(solution)/shard_map/all_to_all | solution.py:442
  23.1 14.0 %all-to-all-done = f32[128,1,1152]{2,1,0:T(1,128)S(1)} async-done(((f32[128,1,1152]{2,1,0:T(1,128)}), f32[128,1,1152]{2,1,0:T(1,128)S(1)}, u32[]{:S(2)}, u32[]{:S(2)}) %all-to-all-start) | async-done | bytes 589856 | tf_op jit(solution)/shard_map/all_to_all | solution.py:442
  37.1 0.0 copy-done.3
  37.1 0.0 copy-done.4
  37.1 0.0 copy-done.2
  37.1 31.7 %render.1 = (f32[3,32,256]{2,1,0:T(8,128)}, f32[384,128]{1,0:T(8,128)S(1)}) custom-call(f32[1152,128]{1,0:T(8,128)S(1)} %bitcast.6, s32[32,4,256]{2,1,0:T(4,128)S(1)} %copy-done.2, f32[3,32,256]{2,1,0:T(8,128)S(1)} %copy-done.3, s32[32]{0:T(128)S(1)} %copy-done.4, s32[1]{0:T(128)} %bitcast.3.rank_ref), custom_call_target="tpu_custom_call" | custom-call | tf_op jit(solution)/shard_map/render/pallas_call | solution.py:469
  68.8 40.6 %all_to_all.18 = f32[128,1,384]{2,1,0:T(1,128)S(1)} all-to-all(f32[128,1,384]{2,1,0:T(1,128)S(1)} %bitcast.10), channel_id=1, replica_groups=mesh['cell'=8,'tile'=16] {'cell','tile'}, dimensions={0} | all-to-all | bytes 393216 | tf_op jit(solution)/shard_map/all_to_all | solution.py:442
  109.3 0.0 copy-done.1
  109.4 0.0 copy-done
  109.4 4.4 %finish.1 = f32[48,8192]{1,0:T(8,128)} custom-call(f32[384,128]{1,0:T(8,128)S(1)} %bitcast.7, s32[128,128]{1,0:T(8,128)S(1)} %bitcast.9, f32[1024,128]{1,0:T(8,128)S(1)} %copy-done), custom_call_target="tpu_custom_call" | custom-call | tf_op jit(solution)/shard_map/finish/pallas_call | solution.py:489
Async XLA Ops:
  0.6 36.4 %copy-start.3 = (f32[3,32,256]{2,1,0:T(8,128)S(1)}, f32[3,32,256]{2,1,0:T(8,128)}, u32[]{:S(2)}) copy-start(f32[3,32,256]{2,1,0:T(8,128)} %cot_ref.1) | copy-start | bytes 294916
  0.6 36.4 %copy-start.4 = (s32[32]{0:T(128)S(1)}, s32[32]{0:T(128)}, u32[]{:S(2)}) copy-start(s32[32]{0:T(128)} %counts_ref.1) | copy-start | bytes 388
  0.7 36.4 %copy-start.2 = (s32[32,4,256]{2,1,0:T(4,128)S(1)}, s32[32,4,256]{2,1,0:T(4,128)}, u32[]{:S(2)}) copy-start(s32[32,4,256]{2,1,0:T(4,128)} %slots_ref.1) | copy-start | bytes 393220
  0.7 108.7 %copy-start.1 = (s32[1,128,128]{2,1,0:T(8,128)S(1)}, s32[1,128,128]{2,1,0:T(8,128)}, u32[]{:S(2)}) copy-start(s32[1,128,128]{2,1,0:T(8,128)} %param.6) | copy-start | bytes 196612
  11.5 97.8 %copy-start = (f32[1024,128]{1,0:T(8,128)S(1)}, f32[1024,128]{1,0:T(8,128)}, u32[]{:S(2)}) copy-start(f32[1024,128]{1,0:T(8,128)} %get-tuple-element.9.basis_ref) | copy-start | bytes 1572868
  11.6 25.5 %all-to-all-start = ((f32[128,1,1152]{2,1,0:T(1,128)}), f32[128,1,1152]{2,1,0:T(1,128)S(1)}, u32[]{:S(2)}, u32[]{:S(2)}) async-start(f32[128,1,1152]{2,1,0:T(1,128)} %bitcast.11), calls=%async_computation | async-start | bytes 1179648 | tf_op jit(solution)/shard_map/all_to_all | solution.py:442

commit v3 on v2

--- a/solution.py
+++ b/solution.py
@@ -15,6 +15,7 @@
 PARAMS = 59
 ATTRS = 9
 UNIT = 256
+FORM = (5, 6, 7)
 Q_OWN = OWNED // UNIT
 Q_SLOT = SLOTS // UNIT
 LANES = 128
@@ -123,10 +124,10 @@
         colour[1],
         centre_u,
         centre_v,
+        log_opacity,
         entry_c / determinant,
         -entry_b / determinant,
         entry_a / determinant,
-        log_opacity,
         colour[2],
     ]
     kept = [jnp.where(value == value, jnp.clip(value, -1e30, 1e30), 0.0) for value in attributes]
@@ -146,41 +147,52 @@
     return high, (values - high.astype(F32)).astype(BF16)
 
 
-def build_table(rows_ref, table_ref, groups):
-    inner = lax.broadcasted_iota(jnp.int32, (16, UNIT), 0) & 7
-    for pair in range(groups // 2):
-        part, ninth = [], []
-        for q in (2 * pair, 2 * pair + 1):
-            halves = [rows_ref[pl.ds(18 * q, 8), :], rows_ref[pl.ds(18 * q + 9, 8), :]]
-            part.append(jnp.concatenate(halves, axis=1))
-            halves = [rows_ref[pl.ds(18 * q + 8, 1), :], rows_ref[pl.ds(18 * q + 17, 1), :]]
-            ninth.append(jnp.broadcast_to(jnp.concatenate(halves, axis=1), (8, UNIT)))
-        first, second, third = split_three(jnp.concatenate(part, axis=0))
-        high, low = split_two(jnp.concatenate(ninth, axis=0))
-        tail = jnp.where(
-            inner == 0, high.astype(F32), jnp.where(inner == 1, low.astype(F32), third.astype(F32))
-        ).astype(BF16)
-        for index, piece in enumerate((first, second, tail)):
-            table_ref[pl.ds(8 * groups * index + 16 * pair, 16), :] = piece
-
-
 def one_hot(low_index):
     rows = lax.broadcasted_iota(jnp.int32, (UNIT, UNIT), 0)
     return jnp.where(rows == low_index, 1.0, 0.0).astype(BF16)
 
 
+def build_table(rows_ref, table_ref, groups):
+    nothing = jnp.zeros((1, UNIT), F32)
+    for pair in range(groups // 2):
+        firsts, seconds = [], []
+        for q in (2 * pair, 2 * pair + 1):
+            halves = [rows_ref[pl.ds(18 * q + 9 * half, 9), :] for half in range(2)]
+            both = jnp.concatenate(halves, axis=1)
+            wanted = jnp.concatenate([both[:5], both[8:9]], axis=0)
+            first, second, third = (part.astype(F32) for part in split_three(wanted))
+            firsts += [first, third[2:4]]
+            seconds += [second, third[4:5], nothing]
+        for index, pieces in enumerate((firsts, seconds)):
+            table_ref[pl.ds(8 * groups * index + 16 * pair, 16), :] = jnp.concatenate(pieces, axis=0).astype(BF16)
+
+
 def gather_block(entries, table_ref, groups):
     every = jnp.dot(table_ref[...], one_hot(entries & (UNIT - 1)), preferred_element_type=F32)
     high_rows = jnp.broadcast_to(entries >> 8, (8, UNIT))
-    picked = [jnp.zeros((8, UNIT), F32)] * 3
+    picked = [jnp.zeros((8, UNIT), F32)] * 2
     for q in range(groups):
         member = high_rows == q
-        for index in range(3):
+        for index in range(2):
             start = 8 * groups * index + 8 * q
             picked[index] = jnp.where(member, every[start : start + 8], picked[index])
-    inner = lax.broadcasted_iota(jnp.int32, (8, UNIT), 0)
-    tail = picked[2]
-    return picked[0] + (picked[1] + jnp.where(inner < 2, 0.0, tail)), tail[0:1] + tail[1:2]
+    thirds = jnp.concatenate(
+        [jnp.zeros((2, UNIT), F32), picked[0][6:8], picked[1][6:7], jnp.zeros((3, UNIT), F32)], axis=0
+    )
+    return (picked[0] + picked[1]) + thirds
+
+
+def gather_lanes(entries, rows_ref, attributes, count):
+    lane = entries & (LANES - 1)
+    high = entries >> 7
+    picked = [jnp.zeros((8, LANES), F32) for a in attributes]
+    for k in range(count):
+        member = high == k
+        for index, a in enumerate(attributes):
+            row = jnp.broadcast_to(rows_ref[pl.ds(ATTRS * k + a, 1), :], (8, LANES))
+            found = jnp.take_along_axis(row, lane, axis=1, mode="promise_in_bounds")
+            picked[index] = jnp.where(member, found, picked[index])
+    return picked
 
 
 def scatter_terms(entries, values, groups):
@@ -235,21 +247,26 @@
 
     def blocks(i, carry):
         index_rows = index_ref[pl.ds(pl.multiple_of(2 * OWN_UNROLL * i, 8), 2 * OWN_UNROLL), :]
+        base = pl.multiple_of(i * (18 * OWN_UNROLL), 8)
+        for group in range(OWN_UNROLL // 4):
+            found = gather_lanes(index_rows[8 * group : 8 * group + 8], rows_ref, FORM, OWNED // LANES)
+            for a, values in zip(FORM, found):
+                send_ref[pl.ds(base + 8 * ATTRS * group + a, 8, stride=ATTRS), :] = values
         for j in range(OWN_UNROLL):
             entries = jnp.concatenate([index_rows[2 * j : 2 * j + 1], index_rows[2 * j + 1 : 2 * j + 2]], axis=1)
-            picked, ninth = gather_block(entries, table_ref, Q_OWN)
+            picked = gather_block(entries, table_ref, Q_OWN)
             for half in range(2):
-                row = pl.multiple_of(i * (18 * OWN_UNROLL), 8) + 18 * j + 9 * half
+                row = base + 18 * j + 9 * half
                 lanes = slice(LANES * half, LANES * half + LANES)
-                send_ref[pl.ds(row, 8), :] = picked[:, lanes]
-                send_ref[pl.ds(row + 8, 1), :] = ninth[:, lanes]
+                send_ref[pl.ds(row, 5), :] = picked[:5, lanes]
+                send_ref[pl.ds(row + 8, 1), :] = picked[5:6, lanes]
         return carry
 
     lax.fori_loop(0, PEERS // 2 // OWN_UNROLL, blocks, 0)
 
 
 GATHER_UNROLL = 8
-RENDER_UNROLL = 4
+RENDER_UNROLL = 8
 MOST = TILE_DEV * BLOCKS
 LISTED = MOST + 8
 
@@ -266,7 +283,8 @@
     triangle_ref,
     entries_ref,
     attr_ref,
-    attr_ninth_ref,
+    halves_ref,
+    form_ref,
     gone_ref,
     total_ref,
     picture_ref,
@@ -285,7 +303,10 @@
 
         def list_block(b, n):
             listed[n] = t * 8 + b
-            entries_ref[n] = slots_ref[t, pl.ds(b, 1), :]
+            row = slots_ref[t, pl.ds(b, 1), :]
+            entries_ref[n] = row
+            halves_ref[pl.ds(2 * n, 1), :] = row[:, :LANES]
+            halves_ref[pl.ds(2 * n + 1, 1), :] = row[:, LANES:]
             return n + 1
 
         return lax.fori_loop(0, count, list_block, n)
@@ -294,13 +315,17 @@
     for extra in range(8):
         listed[live + extra] = TILE_DEV * 8
         entries_ref[live + extra] = jnp.zeros((1, UNIT), jnp.int32)
+        halves_ref[pl.ds(2 * (live + extra), 2), :] = jnp.zeros((2, LANES), jnp.int32)
 
     def gather_step(i, carry):
+        for group in range(GATHER_UNROLL // 4):
+            row = pl.multiple_of(i * (2 * GATHER_UNROLL), 8) + 8 * group
+            found = gather_lanes(halves_ref[pl.ds(row, 8), :], received, FORM, PEERS)
+            for index in range(3):
+                form_ref[index, pl.ds(row, 8), :] = found[index]
         for j in range(GATHER_UNROLL):
             n = i * GATHER_UNROLL + j
-            picked, ninth = gather_block(entries_ref[n], table_ref, Q_SLOT)
-            attr_ref[n] = picked
-            attr_ninth_ref[n] = ninth
+            attr_ref[n] = gather_block(entries_ref[n], table_ref, Q_SLOT)
         return carry
 
     lax.fori_loop(0, (live + GATHER_UNROLL - 1) // GATHER_UNROLL, gather_step, 0)
@@ -323,10 +348,14 @@
             return jnp.broadcast_to(picked[row : row + 1], (8, UNIT))
 
         centre_u, centre_v = wide(2), wide(3)
-        form_a = wide(4) * (-0.5 * LOG2E)
-        form_b = wide(5) * (-LOG2E)
-        form_c = wide(6) * (-0.5 * LOG2E)
-        log_opacity = wide(7)
+        def form(index):
+            halves = [form_ref[index, pl.ds(2 * n + half, 1), :] for half in range(2)]
+            return jnp.broadcast_to(jnp.concatenate(halves, axis=1), (8, UNIT))
+
+        form_a = form(0) * (-0.5 * LOG2E)
+        form_b = form(1) * (-LOG2E)
+        form_c = form(2) * (-0.5 * LOG2E)
+        log_opacity = wide(4)
         constant, linear = [], []
         for half in range(2):
             delta_x = (across + (origin_x + 8.0 * half)) - centre_u
@@ -359,7 +388,7 @@
                     back[c][half] += column * weight[:, LANES * half : LANES * half + LANES]
             weights.append(weight)
         weight_high, weight_low = split_two(jnp.concatenate(weights, axis=0))
-        columns = jnp.concatenate([picked[0:2], attr_ninth_ref[n], lane_ones], axis=0)
+        columns = jnp.concatenate([picked[0:2], picked[5:6], lane_ones], axis=0)
         colour_high, colour_low = split_two(columns)
         nothing = jnp.zeros((8, UNIT), BF16)
         left = jnp.concatenate(
@@ -457,7 +486,7 @@
         scratch_shapes=[
             pltpu.VMEM((PAD_PARAMS * OWNED // LANES, LANES), F32),
             pltpu.VMEM((ATTRS * OWNED // LANES, LANES), F32),
-            pltpu.VMEM((24 * Q_OWN, UNIT), BF16),
+            pltpu.VMEM((16 * Q_OWN, UNIT), BF16),
             pltpu.VMEM((PEERS, WIDTH), jnp.int32),
             pltpu.SemaphoreType.DMA((OWNED // LANES,)),
             pltpu.SemaphoreType.DMA(()),
@@ -472,11 +501,12 @@
         in_specs=[vmem, vmem, vmem, smem, smem],
         out_specs=(vmem, vmem),
         scratch_shapes=[
-            pltpu.VMEM((24 * Q_SLOT, UNIT), BF16),
+            pltpu.VMEM((16 * Q_SLOT, UNIT), BF16),
             pltpu.VMEM((UNIT, UNIT), BF16),
             pltpu.VMEM((LISTED, 1, UNIT), jnp.int32),
             pltpu.VMEM((LISTED, 8, UNIT), F32),
-            pltpu.VMEM((LISTED, 1, UNIT), F32),
+            pltpu.VMEM((2 * LISTED, LANES), jnp.int32),
+            pltpu.VMEM((3, 2 * LISTED, LANES), F32),
             pltpu.VMEM((UNIT, LANES), F32),
             pltpu.VMEM((6 * Q_SLOT, UNIT), F32),
             pltpu.VMEM((TILE_DEV + 1, 8, UNIT), F32),

time: 115 us -> 104 us (0.904)
  blocking collectives: 40.6 us -> 25.6 us
  Pallas kernels: 46.9 us -> 52 us
    all_to_all x1, blocking collectives: 40.6 us -> 25.6 us  [exchange(): return lax.all_to_all(buffer, AXES, split_axis=0, concat_axis=0, tiled=True)]
    pallas_call x1, Pallas kernels: 31.7 us -> 38.4 us  [per_device(): pl.pallas_call(render_kernel, out_shape=(shape((3, TILE_DEV, UNIT), F32),...]
    pallas_call x1, Pallas kernels: 10.9 us -> 9.32 us  [per_device(): pl.pallas_call(own_kernel, out_shape=(shape((ATTRS * PEERS, WIDTH), F32),...]
where the time goes in v3:
time: 104 us
  Pallas kernels  52 us (50%)
  blocking collectives  25.6 us (25%)
  waiting for transfers between devices  14 us (13%)
  starting transfers between devices  11.5 us (11%)
    pallas_call x1, Pallas kernels, per_device(): pl.pallas_call(render_kernel, out_shape=(shape((3, TILE_DEV, UNIT), F32),...  38.4 us
    all_to_all x1, blocking collectives, exchange(): return lax.all_to_all(buffer, AXES, split_axis=0, concat_axis=0, tiled=True)  25.6 us
    all_to_all x1, waiting for transfers between devices, exchange(): return lax.all_to_all(buffer, AXES, split_axis=0, concat_axis=0, tiled=True)  14 us
    all_to_all x1, starting transfers between devices, exchange(): return lax.all_to_all(buffer, AXES, split_axis=0, concat_axis=0, tiled=True)  11.5 us
    pallas_call x1, Pallas kernels, per_device(): pl.pallas_call(own_kernel, out_shape=(shape((ATTRS * PEERS, WIDTH), F32),...  9.32 us
    pallas_call x1, Pallas kernels, per_device(): pl.pallas_call(finish_kernel, out_shape=shape((48, OWNED), F32), in_specs...  4.37 us
  transfers between devices with their start and end apart: 1, of which 1 were waited for; matrix products, arithmetic and copies ran while one was open for 0% of the time, Pallas kernels for 0%

profile of v3, /device:TPU:1, one launch (start us, length us, event | category | flops | bytes accessed | tf_op | source)
XLA Modules:
  0.0 103.9 jit_solution(17554574936483518248)
XLA Ops:
  0.6 0.0 copy-start.3
  0.6 0.0 copy-start.4
  0.7 0.0 copy-start.2
  0.7 0.0 copy-start.1
  0.7 9.3 %project_and_pack.1 = (f32[1152,128]{1,0:T(8,128)}, f32[1024,128]{1,0:T(8,128)}) custom-call(f32[59,8192]{1,0:T(8,128)} %gaussians.1, s32[128,128]{1,0:T(8,128)} %bitcast.8), custom_call_target="tpu_custom_call" | custom-call | tf_op jit(solution)/shard_map/project_and_pack/pallas_call | solution.py:481
  10.0 0.0 copy-start
  10.0 11.5 %all-to-all-start = ((f32[128,1,1152]{2,1,0:T(1,128)}), f32[128,1,1152]{2,1,0:T(1,128)S(1)}, u32[]{:S(2)}, u32[]{:S(2)}) async-start(f32[128,1,1152]{2,1,0:T(1,128)} %bitcast.11), calls=%async_computation | async-start | bytes 1179648 | tf_op jit(solution)/shard_map/all_to_all | solution.py:471
  21.5 14.0 %all-to-all-done = f32[128,1,1152]{2,1,0:T(1,128)S(1)} async-done(((f32[128,1,1152]{2,1,0:T(1,128)}), f32[128,1,1152]{2,1,0:T(1,128)S(1)}, u32[]{:S(2)}, u32[]{:S(2)}) %all-to-all-start) | async-done | bytes 589856 | tf_op jit(solution)/shard_map/all_to_all | solution.py:471
  35.5 0.0 copy-done.3
  35.5 0.0 copy-done.4
  35.5 0.0 copy-done.2
  35.5 38.4 %render.1 = (f32[3,32,256]{2,1,0:T(8,128)}, f32[384,128]{1,0:T(8,128)S(1)}) custom-call(f32[1152,128]{1,0:T(8,128)S(1)} %bitcast.6, s32[32,4,256]{2,1,0:T(4,128)S(1)} %copy-done.2, f32[3,32,256]{2,1,0:T(8,128)S(1)} %copy-done.3, s32[32]{0:T(128)S(1)} %copy-done.4, s32[1]{0:T(128)} %bitcast.3.rank_ref), custom_call_target="tpu_custom_call" | custom-call | tf_op jit(solution)/shard_map/render/pallas_call | solution.py:498
  73.9 25.6 %all_to_all.18 = f32[128,1,384]{2,1,0:T(1,128)S(1)} all-to-all(f32[128,1,384]{2,1,0:T(1,128)S(1)} %bitcast.10), channel_id=1, replica_groups=mesh['cell'=8,'tile'=16] {'cell','tile'}, dimensions={0} | all-to-all | bytes 393216 | tf_op jit(solution)/shard_map/all_to_all | solution.py:471
  99.5 0.0 copy-done.1
  99.5 0.0 copy-done
  99.5 4.4 %finish.1 = f32[48,8192]{1,0:T(8,128)} custom-call(f32[384,128]{1,0:T(8,128)S(1)} %bitcast.7, s32[128,128]{1,0:T(8,128)S(1)} %bitcast.9, f32[1024,128]{1,0:T(8,128)S(1)} %copy-done), custom_call_target="tpu_custom_call" | custom-call | tf_op jit(solution)/shard_map/finish/pallas_call | solution.py:519
Async XLA Ops:
  0.6 34.9 %copy-start.3 = (f32[3,32,256]{2,1,0:T(8,128)S(1)}, f32[3,32,256]{2,1,0:T(8,128)}, u32[]{:S(2)}) copy-start(f32[3,32,256]{2,1,0:T(8,128)} %cot_ref.1) | copy-start | bytes 294916
  0.6 34.9 %copy-start.4 = (s32[32]{0:T(128)S(1)}, s32[32]{0:T(128)}, u32[]{:S(2)}) copy-start(s32[32]{0:T(128)} %counts_ref.1) | copy-start | bytes 388
  0.7 34.9 %copy-start.2 = (s32[32,4,256]{2,1,0:T(4,128)S(1)}, s32[32,4,256]{2,1,0:T(4,128)}, u32[]{:S(2)}) copy-start(s32[32,4,256]{2,1,0:T(4,128)} %slots_ref.1) | copy-start | bytes 393220
  0.7 98.8 %copy-start.1 = (s32[1,128,128]{2,1,0:T(8,128)S(1)}, s32[1,128,128]{2,1,0:T(8,128)}, u32[]{:S(2)}) copy-start(s32[1,128,128]{2,1,0:T(8,128)} %param.6) | copy-start | bytes 196612
  10.0 89.5 %copy-start = (f32[1024,128]{1,0:T(8,128)S(1)}, f32[1024,128]{1,0:T(8,128)}, u32[]{:S(2)}) copy-start(f32[1024,128]{1,0:T(8,128)} %get-tuple-element.9.basis_ref) | copy-start | bytes 1572868
  10.0 25.5 %all-to-all-start = ((f32[128,1,1152]{2,1,0:T(1,128)}), f32[128,1,1152]{2,1,0:T(1,128)S(1)}, u32[]{:S(2)}, u32[]{:S(2)}) async-start(f32[128,1,1152]{2,1,0:T(1,128)} %bitcast.11), calls=%async_computation | async-start | bytes 1179648 | tf_op jit(solution)/shard_map/all_to_all | solution.py:471

commit v4 on v3

--- a/solution.py
+++ b/solution.py
@@ -298,20 +298,15 @@
     picture_ref[...] = jnp.zeros_like(picture_ref)
     total_ref[...] = jnp.zeros_like(total_ref)
 
-    def list_tile(t, n):
-        count = counts_ref[t]
-
-        def list_block(b, n):
-            listed[n] = t * 8 + b
+    live = jnp.int32(0)
+    for t in range(TILE_DEV):
+        for b in range(BLOCKS):
+            listed[live + b] = t * 8 + b
             row = slots_ref[t, pl.ds(b, 1), :]
-            entries_ref[n] = row
-            halves_ref[pl.ds(2 * n, 1), :] = row[:, :LANES]
-            halves_ref[pl.ds(2 * n + 1, 1), :] = row[:, LANES:]
-            return n + 1
-
-        return lax.fori_loop(0, count, list_block, n)
-
-    live = lax.fori_loop(0, TILE_DEV, list_tile, 0)
+            entries_ref[live + b] = row
+            for half in range(2):
+                halves_ref[pl.ds(2 * (live + b) + half, 1), :] = row[:, LANES * half : LANES * half + LANES]
+        live = live + counts_ref[t]
     for extra in range(8):
         listed[live + extra] = TILE_DEV * 8
         entries_ref[live + extra] = jnp.zeros((1, UNIT), jnp.int32)
@@ -371,7 +366,7 @@
         log_keep = jnp.log2(1.0 - alpha)
         sums = jnp.dot(jnp.concatenate(split_two(log_keep), axis=0), triangle_ref[...], preferred_element_type=F32)
         cot = jnp.concatenate([cot_ref[c, pl.ds(source, 1), :] for c in range(3)] + [lane_ones], axis=0)
-        cot_columns = jnp.transpose(cot)
+        cot_columns = [jnp.transpose(jnp.broadcast_to(cot[c : c + 1], (LANES, UNIT))) for c in range(3)]
         kept = jnp.where(first, 0.0, 1.0)
         back = [[jnp.zeros((8, LANES), F32) for half in range(2)] for c in range(3)]
         weights = []
@@ -382,11 +377,12 @@
             weight = alpha[rows] * jnp.exp2(earlier)
             last = (earlier + log_keep[rows])[:, UNIT - 1 : UNIT]
             gone_ref[pl.ds(8 * p, 8), :] = jnp.broadcast_to(last, (8, LANES))
-            for c in range(3):
-                column = jnp.broadcast_to(cot_columns[rows, c : c + 1], (8, LANES))
+            weights.append(weight)
+        for c in range(3):
+            for p in range(UNIT // 8):
+                column = cot_columns[c][8 * p : 8 * p + 8]
                 for half in range(2):
-                    back[c][half] += column * weight[:, LANES * half : LANES * half + LANES]
-            weights.append(weight)
+                    back[c][half] += column * weights[p][:, LANES * half : LANES * half + LANES]
         weight_high, weight_low = split_two(jnp.concatenate(weights, axis=0))
         columns = jnp.concatenate([picked[0:2], picked[5:6], lane_ones], axis=0)
         colour_high, colour_low = split_two(columns)

time: 104 us -> 101 us (0.971)
  Pallas kernels: 52 us -> 42.1 us
  blocking collectives: 25.6 us -> 32.9 us
    pallas_call x1, Pallas kernels: 38.4 us -> 28.4 us  [per_device(): pl.pallas_call(render_kernel, out_shape=(shape((3, TILE_DEV, UNIT), F32),...]
    all_to_all x1, blocking collectives: 25.6 us -> 32.9 us  [exchange(): return lax.all_to_all(buffer, AXES, split_axis=0, concat_axis=0, tiled=True)]
where the time goes in v4:
time: 101 us
  Pallas kernels  42.1 us (42%)
  blocking collectives  32.9 us (33%)
  waiting for transfers between devices  14 us (14%)
  starting transfers between devices  11.5 us (11%)
    all_to_all x1, blocking collectives, exchange(): return lax.all_to_all(buffer, AXES, split_axis=0, concat_axis=0, tiled=True)  32.9 us
    pallas_call x1, Pallas kernels, per_device(): pl.pallas_call(render_kernel, out_shape=(shape((3, TILE_DEV, UNIT), F32),...  28.4 us
    all_to_all x1, waiting for transfers between devices, exchange(): return lax.all_to_all(buffer, AXES, split_axis=0, concat_axis=0, tiled=True)  14 us
    all_to_all x1, starting transfers between devices, exchange(): return lax.all_to_all(buffer, AXES, split_axis=0, concat_axis=0, tiled=True)  11.5 us
    pallas_call x1, Pallas kernels, per_device(): pl.pallas_call(own_kernel, out_shape=(shape((ATTRS * PEERS, WIDTH), F32),...  9.32 us
    pallas_call x1, Pallas kernels, per_device(): pl.pallas_call(finish_kernel, out_shape=shape((48, OWNED), F32), in_specs...  4.37 us
  transfers between devices with their start and end apart: 1, of which 1 were waited for; matrix products, arithmetic and copies ran while one was open for 0% of the time, Pallas kernels for 0%

profile of v4, /device:TPU:1, one launch (start us, length us, event | category | flops | bytes accessed | tf_op | source)
XLA Modules:
  0.0 101.2 jit_solution(16921411420326409079)
XLA Ops:
  0.6 0.0 copy-start.3
  0.6 0.0 copy-start.4
  0.7 0.0 copy-start.2
  0.7 0.0 copy-start.1
  0.7 9.3 %project_and_pack.1 = (f32[1152,128]{1,0:T(8,128)}, f32[1024,128]{1,0:T(8,128)}) custom-call(f32[59,8192]{1,0:T(8,128)} %gaussians.1, s32[128,128]{1,0:T(8,128)} %bitcast.8), custom_call_target="tpu_custom_call" | custom-call | tf_op jit(solution)/shard_map/project_and_pack/pallas_call | solution.py:477
  10.0 0.0 copy-start
  10.0 11.5 %all-to-all-start = ((f32[128,1,1152]{2,1,0:T(1,128)}), f32[128,1,1152]{2,1,0:T(1,128)S(1)}, u32[]{:S(2)}, u32[]{:S(2)}) async-start(f32[128,1,1152]{2,1,0:T(1,128)} %bitcast.11), calls=%async_computation | async-start | bytes 1179648 | tf_op jit(solution)/shard_map/all_to_all | solution.py:467
  21.5 14.0 %all-to-all-done = f32[128,1,1152]{2,1,0:T(1,128)S(1)} async-done(((f32[128,1,1152]{2,1,0:T(1,128)}), f32[128,1,1152]{2,1,0:T(1,128)S(1)}, u32[]{:S(2)}, u32[]{:S(2)}) %all-to-all-start) | async-done | bytes 589856 | tf_op jit(solution)/shard_map/all_to_all | solution.py:467
  35.5 0.0 copy-done.3
  35.5 0.0 copy-done.4
  35.5 0.0 copy-done.2
  35.5 28.4 %render.1 = (f32[3,32,256]{2,1,0:T(8,128)}, f32[384,128]{1,0:T(8,128)S(1)}) custom-call(f32[1152,128]{1,0:T(8,128)S(1)} %bitcast.6, s32[32,4,256]{2,1,0:T(4,128)S(1)} %copy-done.2, f32[3,32,256]{2,1,0:T(8,128)S(1)} %copy-done.3, s32[32]{0:T(128)S(1)} %copy-done.4, s32[1]{0:T(128)} %bitcast.3.rank_ref), custom_call_target="tpu_custom_call" | custom-call | tf_op jit(solution)/shard_map/render/pallas_call | solution.py:494
  63.9 32.9 %all_to_all.18 = f32[128,1,384]{2,1,0:T(1,128)S(1)} all-to-all(f32[128,1,384]{2,1,0:T(1,128)S(1)} %bitcast.10), channel_id=1, replica_groups=mesh['cell'=8,'tile'=16] {'cell','tile'}, dimensions={0} | all-to-all | bytes 393216 | tf_op jit(solution)/shard_map/all_to_all | solution.py:467
  96.8 0.0 copy-done.1
  96.9 0.0 copy-done
  96.9 4.4 %finish.1 = f32[48,8192]{1,0:T(8,128)} custom-call(f32[384,128]{1,0:T(8,128)S(1)} %bitcast.7, s32[128,128]{1,0:T(8,128)S(1)} %bitcast.9, f32[1024,128]{1,0:T(8,128)S(1)} %copy-done), custom_call_target="tpu_custom_call" | custom-call | tf_op jit(solution)/shard_map/finish/pallas_call | solution.py:515
Async XLA Ops:
  0.6 34.9 %copy-start.3 = (f32[3,32,256]{2,1,0:T(8,128)S(1)}, f32[3,32,256]{2,1,0:T(8,128)}, u32[]{:S(2)}) copy-start(f32[3,32,256]{2,1,0:T(8,128)} %cot_ref.1) | copy-start | bytes 294916
  0.6 34.9 %copy-start.4 = (s32[32]{0:T(128)S(1)}, s32[32]{0:T(128)}, u32[]{:S(2)}) copy-start(s32[32]{0:T(128)} %counts_ref.1) | copy-start | bytes 388
  0.7 34.9 %copy-start.2 = (s32[32,4,256]{2,1,0:T(4,128)S(1)}, s32[32,4,256]{2,1,0:T(4,128)}, u32[]{:S(2)}) copy-start(s32[32,4,256]{2,1,0:T(4,128)} %slots_ref.1) | copy-start | bytes 393220
  0.7 96.2 %copy-start.1 = (s32[1,128,128]{2,1,0:T(8,128)S(1)}, s32[1,128,128]{2,1,0:T(8,128)}, u32[]{:S(2)}) copy-start(s32[1,128,128]{2,1,0:T(8,128)} %param.6) | copy-start | bytes 196612
  10.0 86.9 %copy-start = (f32[1024,128]{1,0:T(8,128)S(1)}, f32[1024,128]{1,0:T(8,128)}, u32[]{:S(2)}) copy-start(f32[1024,128]{1,0:T(8,128)} %get-tuple-element.9.basis_ref) | copy-start | bytes 1572868
  10.0 25.5 %all-to-all-start = ((f32[128,1,1152]{2,1,0:T(1,128)}), f32[128,1,1152]{2,1,0:T(1,128)S(1)}, u32[]{:S(2)}, u32[]{:S(2)}) async-start(f32[128,1,1152]{2,1,0:T(1,128)} %bitcast.11), calls=%async_computation | async-start | bytes 1179648 | tf_op jit(solution)/shard_map/all_to_all | solution.py:467

commit v5 on v4

--- a/solution.py
+++ b/solution.py
@@ -265,10 +265,10 @@
     lax.fori_loop(0, PEERS // 2 // OWN_UNROLL, blocks, 0)
 
 
-GATHER_UNROLL = 8
+GATHER_UNROLL = 16
 RENDER_UNROLL = 8
 MOST = TILE_DEV * BLOCKS
-LISTED = MOST + 8
+LISTED = MOST + 16
 
 
 def render_kernel(
@@ -307,7 +307,7 @@
             for half in range(2):
                 halves_ref[pl.ds(2 * (live + b) + half, 1), :] = row[:, LANES * half : LANES * half + LANES]
         live = live + counts_ref[t]
-    for extra in range(8):
+    for extra in range(16):
         listed[live + extra] = TILE_DEV * 8
         entries_ref[live + extra] = jnp.zeros((1, UNIT), jnp.int32)
         halves_ref[pl.ds(2 * (live + extra), 2), :] = jnp.zeros((2, LANES), jnp.int32)

time: 101 us -> 100 us (0.990)
  blocking collectives: 32.9 us -> 31.5 us
    all_to_all x1, blocking collectives: 32.9 us -> 31.5 us  [exchange(): return lax.all_to_all(buffer, AXES, split_axis=0, concat_axis=0, tiled=True)]
where the time goes in v5:
time: 100 us
  Pallas kernels  42.6 us (43%)
  blocking collectives  31.5 us (32%)
  waiting for transfers between devices  14 us (14%)
  starting transfers between devices  11.5 us (12%)
    all_to_all x1, blocking collectives, exchange(): return lax.all_to_all(buffer, AXES, split_axis=0, concat_axis=0, tiled=True)  31.5 us
    pallas_call x1, Pallas kernels, per_device(): pl.pallas_call(render_kernel, out_shape=(shape((3, TILE_DEV, UNIT), F32),...  29 us
    all_to_all x1, waiting for transfers between devices, exchange(): return lax.all_to_all(buffer, AXES, split_axis=0, concat_axis=0, tiled=True)  14 us
    all_to_all x1, starting transfers between devices, exchange(): return lax.all_to_all(buffer, AXES, split_axis=0, concat_axis=0, tiled=True)  11.5 us
    pallas_call x1, Pallas kernels, per_device(): pl.pallas_call(own_kernel, out_shape=(shape((ATTRS * PEERS, WIDTH), F32),...  9.32 us
    pallas_call x1, Pallas kernels, per_device(): pl.pallas_call(finish_kernel, out_shape=shape((48, OWNED), F32), in_specs...  4.37 us
  transfers between devices with their start and end apart: 1, of which 1 were waited for; matrix products, arithmetic and copies ran while one was open for 0% of the time, Pallas kernels for 0%

profile of v5, /device:TPU:1, one launch (start us, length us, event | category | flops | bytes accessed | tf_op | source)
XLA Modules:
  0.0 100.4 jit_solution(12424574205206222928)
XLA Ops:
  0.6 0.0 copy-start.3
  0.6 0.0 copy-start.4
  0.7 0.0 copy-start.2
  0.7 0.0 copy-start.1
  0.7 9.3 %project_and_pack.1 = (f32[1152,128]{1,0:T(8,128)}, f32[1024,128]{1,0:T(8,128)}) custom-call(f32[59,8192]{1,0:T(8,128)} %gaussians.1, s32[128,128]{1,0:T(8,128)} %bitcast.8), custom_call_target="tpu_custom_call" | custom-call | tf_op jit(solution)/shard_map/project_and_pack/pallas_call | solution.py:477
  10.0 0.0 copy-start
  10.0 11.5 %all-to-all-start = ((f32[128,1,1152]{2,1,0:T(1,128)}), f32[128,1,1152]{2,1,0:T(1,128)S(1)}, u32[]{:S(2)}, u32[]{:S(2)}) async-start(f32[128,1,1152]{2,1,0:T(1,128)} %bitcast.11), calls=%async_computation | async-start | bytes 1179648 | tf_op jit(solution)/shard_map/all_to_all | solution.py:467
  21.5 14.0 %all-to-all-done = f32[128,1,1152]{2,1,0:T(1,128)S(1)} async-done(((f32[128,1,1152]{2,1,0:T(1,128)}), f32[128,1,1152]{2,1,0:T(1,128)S(1)}, u32[]{:S(2)}, u32[]{:S(2)}) %all-to-all-start) | async-done | bytes 589856 | tf_op jit(solution)/shard_map/all_to_all | solution.py:467
  35.5 0.0 copy-done.3
  35.5 0.0 copy-done.4
  35.5 0.0 copy-done.2
  35.5 29.0 %render.1 = (f32[3,32,256]{2,1,0:T(8,128)}, f32[384,128]{1,0:T(8,128)S(1)}) custom-call(f32[1152,128]{1,0:T(8,128)S(1)} %bitcast.6, s32[32,4,256]{2,1,0:T(4,128)S(1)} %copy-done.2, f32[3,32,256]{2,1,0:T(8,128)S(1)} %copy-done.3, s32[32]{0:T(128)S(1)} %copy-done.4, s32[1]{0:T(128)} %bitcast.3.rank_ref), custom_call_target="tpu_custom_call" | custom-call | tf_op jit(solution)/shard_map/render/pallas_call | solution.py:494
  64.5 31.5 %all_to_all.18 = f32[128,1,384]{2,1,0:T(1,128)S(1)} all-to-all(f32[128,1,384]{2,1,0:T(1,128)S(1)} %bitcast.10), channel_id=1, replica_groups=mesh['cell'=8,'tile'=16] {'cell','tile'}, dimensions={0} | all-to-all | bytes 393216 | tf_op jit(solution)/shard_map/all_to_all | solution.py:467
  96.0 0.0 copy-done.1
  96.0 0.0 copy-done
  96.0 4.4 %finish.1 = f32[48,8192]{1,0:T(8,128)} custom-call(f32[384,128]{1,0:T(8,128)S(1)} %bitcast.7, s32[128,128]{1,0:T(8,128)S(1)} %bitcast.9, f32[1024,128]{1,0:T(8,128)S(1)} %copy-done), custom_call_target="tpu_custom_call" | custom-call | tf_op jit(solution)/shard_map/finish/pallas_call | solution.py:515
Async XLA Ops:
  0.6 34.9 %copy-start.3 = (f32[3,32,256]{2,1,0:T(8,128)S(1)}, f32[3,32,256]{2,1,0:T(8,128)}, u32[]{:S(2)}) copy-start(f32[3,32,256]{2,1,0:T(8,128)} %cot_ref.1) | copy-start | bytes 294916
  0.6 34.9 %copy-start.4 = (s32[32]{0:T(128)S(1)}, s32[32]{0:T(128)}, u32[]{:S(2)}) copy-start(s32[32]{0:T(128)} %counts_ref.1) | copy-start | bytes 388
  0.7 34.9 %copy-start.2 = (s32[32,4,256]{2,1,0:T(4,128)S(1)}, s32[32,4,256]{2,1,0:T(4,128)}, u32[]{:S(2)}) copy-start(s32[32,4,256]{2,1,0:T(4,128)} %slots_ref.1) | copy-start | bytes 393220
  0.7 95.3 %copy-start.1 = (s32[1,128,128]{2,1,0:T(8,128)S(1)}, s32[1,128,128]{2,1,0:T(8,128)}, u32[]{:S(2)}) copy-start(s32[1,128,128]{2,1,0:T(8,128)} %param.6) | copy-start | bytes 196612
  10.0 86.0 %copy-start = (f32[1024,128]{1,0:T(8,128)S(1)}, f32[1024,128]{1,0:T(8,128)}, u32[]{:S(2)}) copy-start(f32[1024,128]{1,0:T(8,128)} %get-tuple-element.9.basis_ref) | copy-start | bytes 1572868
  10.0 25.5 %all-to-all-start = ((f32[128,1,1152]{2,1,0:T(1,128)}), f32[128,1,1152]{2,1,0:T(1,128)S(1)}, u32[]{:S(2)}, u32[]{:S(2)}) async-start(f32[128,1,1152]{2,1,0:T(1,128)} %bitcast.11), calls=%async_computation | async-start | bytes 1179648 | tf_op jit(solution)/shard_map/all_to_all | solution.py:467
